TPU v7x, 256 devices: a whole 4x4x8 slice. The times are simulated.
256 devices in a mesh: tm: 128 (over x, z, y_lo, core), batch: 2 (over y_hi).
Axes of the slice: x: 4, y: 4 (y_hi: 2, y_lo: 2; y = y_hi * 2 + y_lo), z: 8, core: 2. Of those that a mesh axis runs over, the one named last changes fastest.
Arguments:
- stem_pre: bfloat16 [2, 16384, 1280], P('batch', 'tm'), may hold values from -6 to 6
- attention_norm_gain: float32 [1280], replicated, may hold values from 0.5 to 1.5
- attention_norm_bias: float32 [1280], replicated, may hold values from -3 to 3
- w_attn: bfloat16 [1280, 2560], replicated, may hold values from -0.15625 to 0.15625
- queries: bfloat16 [2, 16384, 640], P('batch', 'tm'), may hold values from -10 to 10
- keys: bfloat16 [2, 16384, 640], P('batch', 'tm'), may hold values from -4 to 4
- values: bfloat16 [2, 16384, 640], P('batch', 'tm'), may hold values from -6 to 6
- grad_out: bfloat16 [2, 16384, 1280], P('batch', 'tm'), may hold values from -24 to 24
- frames: int32 [2, 8], P('batch'), may hold values from 2048 to 4096, as said below
Outputs:
- grad_stem: bfloat16 [2, 16384, 1280], P('batch', 'tm')
- grad_attn: float32 [1280, 2560], P('tm')
- ln_grads: float32 [2, 1280], replicated
Inputs may be any that keep to these rules, and one draw needn't show every extreme that they name: `frames`: one entry per recording, batch row first.
All inputs are finite; a program needn't handle non-finite values.
Results may differ from a plain program's by a relative error of at most 0.02.
Values may be sent and summed in bfloat16 or wider, within the bound.
A program may use at most 128 MiB of HBM per device.

v0:
```python
import math

import jax
import jax.numpy as jnp
from jax import lax
from jax.sharding import PartitionSpec as P

HEAD_DIM = 64
HEADS = 10
SPAN = 16


NEG_FILL = -1e30
EPSILON = 1e-05


def swapped(array, axis, stride):
    return lax.ppermute(array, axis, [(i, i ^ 1 << stride) for i in range(lax.axis_size(axis))])


def gelu_and_slope(stem_in):
    normal_cdf = 0.5 * (1.0 + lax.erf(stem_in / math.sqrt(2.0)))
    density = jnp.exp(-0.5 * stem_in * stem_in) / math.sqrt(2.0 * math.pi)
    return (stem_in * normal_cdf, normal_cdf + stem_in * density)


def sinusoid(positions, features):
    half_width = features // 2
    frequency = jnp.exp(
        -math.log(10000.0) / (half_width - 1) * jnp.arange(half_width, dtype=jnp.float32)
    )
    angles = positions[:, None] * frequency[None, :]
    return jnp.concatenate([jnp.sin(angles), jnp.cos(angles)], axis=1)


def masked_scores(query_heads, key_heads, key_valid):
    scale = 1.0 / math.sqrt(HEAD_DIM)
    scores = (
        jnp.einsum("qhd,khd->hqk", query_heads, key_heads, preferred_element_type=jnp.float32)
        * scale
    )
    return jnp.where(key_valid[None, None, :], scores, NEG_FILL)


def local(
    stem_pre,
    attention_norm_gain,
    attention_norm_bias,
    w_attn,
    queries,
    keys,
    values,
    grad_out,
    frames,
):
    tok_rows = stem_pre.shape[1]
    features = stem_pre.shape[2]
    head_width = queries.shape[2]
    scale = 1.0 / math.sqrt(HEAD_DIM)
    bit_count = SPAN.bit_length() - 1
    group_slot = lax.axis_index("tm") % SPAN
    group_index = lax.axis_index("tm") // SPAN
    frame_limit = jnp.sum(jnp.where(jnp.arange(frames.shape[1]) == group_index, frames[0], 0))
    offset = group_slot * tok_rows
    stem_in = stem_pre[0].astype(jnp.float32)
    activated, gelu_slope = gelu_and_slope(stem_in)
    positions = (offset + jnp.arange(tok_rows)).astype(jnp.float32)
    embedded = activated + sinusoid(positions, features)
    row_mean = jnp.mean(embedded, axis=1, keepdims=True)
    centered_input = embedded - row_mean
    inverse_deviation = lax.rsqrt(
        jnp.mean(centered_input * centered_input, axis=1, keepdims=True) + EPSILON
    )
    standardized_input = centered_input * inverse_deviation
    normalized_input = (standardized_input * attention_norm_gain + attention_norm_bias).astype(
        jnp.bfloat16
    )
    incoming_gradient = grad_out[0]
    grad_heads = jnp.dot(
        incoming_gradient, w_attn[:, 3 * head_width :], preferred_element_type=jnp.float32
    ).astype(jnp.bfloat16)
    own_query = queries[0]
    own_key = keys[0]
    own_value = values[0]
    gathered = jnp.concatenate([own_key, own_value], axis=1)
    for bit_index in range(bit_count):
        partner = swapped(gathered, "tm", bit_index)
        is_upper = group_slot >> bit_index & 1 == 1
        gathered = jnp.where(
            is_upper,
            jnp.concatenate([partner, gathered], axis=0),
            jnp.concatenate([gathered, partner], axis=0),
        )
    key_count = gathered.shape[0]
    key_valid = 2 * jnp.arange(key_count) < frame_limit
    key_heads = gathered[:, :head_width].reshape(key_count, HEADS, HEAD_DIM)
    value_heads = gathered[:, head_width:].reshape(key_count, HEADS, HEAD_DIM)
    query_heads = own_query.reshape(tok_rows, HEADS, HEAD_DIM)
    cot_heads = grad_heads.reshape(tok_rows, HEADS, HEAD_DIM)
    scores = masked_scores(query_heads, key_heads, key_valid)
    totals = jax.nn.logsumexp(scores, axis=2)
    attn_prob = jnp.exp(scores - totals[:, :, None])
    prob_bf = attn_prob.astype(jnp.bfloat16)
    attn_out = jnp.einsum(
        "hqk,khd->qhd", prob_bf, value_heads, preferred_element_type=jnp.float32
    ).astype(jnp.bfloat16)
    row_delta = jnp.einsum("qhd,qhd->hq", cot_heads, attn_out, preferred_element_type=jnp.float32)
    grad_prob = jnp.einsum(
        "qhd,khd->hqk", cot_heads, value_heads, preferred_element_type=jnp.float32
    )
    dscore = (attn_prob * (grad_prob - row_delta[:, :, None]) * scale).astype(jnp.bfloat16)
    grad_query = jnp.einsum(
        "hqk,khd->qhd", dscore, key_heads, preferred_element_type=jnp.float32
    ).reshape(tok_rows, head_width)
    attn_out = attn_out.reshape(tok_rows, head_width)
    grad_key_all = jnp.einsum(
        "hqk,qhd->khd", dscore, query_heads, preferred_element_type=jnp.float32
    )
    grad_value_all = jnp.einsum(
        "hqk,qhd->khd", prob_bf, cot_heads, preferred_element_type=jnp.float32
    )
    key_block = jnp.concatenate(
        [
            grad_key_all.reshape(key_count, head_width),
            grad_value_all.reshape(key_count, head_width),
        ],
        axis=1,
    )
    for bit_index in reversed(range(bit_count)):
        half_rows = key_block.shape[0] // 2
        lower_rows = key_block[:half_rows]
        upper_rows = key_block[half_rows:]
        is_upper = group_slot >> bit_index & 1 == 1
        kept_rows = jnp.where(is_upper, upper_rows, lower_rows)
        sent_rows = jnp.where(is_upper, lower_rows, upper_rows)
        key_block = kept_rows + swapped(sent_rows.astype(jnp.bfloat16), "tm", bit_index).astype(
            sent_rows.dtype
        )
    grad_key = key_block[:, :head_width]
    grad_value = key_block[:, head_width:]
    grad_qkv = jnp.concatenate([grad_query, grad_key, grad_value], axis=1).astype(jnp.bfloat16)
    normalized_gradient = lax.dot_general(
        grad_qkv,
        w_attn[:, : 3 * head_width],
        (((1,), (1,)), ((), ())),
        preferred_element_type=jnp.float32,
    )
    row_share = lax.psum_scatter(
        jnp.concatenate(
            [
                lax.dot_general(
                    normalized_input,
                    grad_qkv,
                    (((0,), (0,)), ((), ())),
                    preferred_element_type=jnp.float32,
                ),
                lax.dot_general(
                    incoming_gradient,
                    attn_out,
                    (((0,), (0,)), ((), ())),
                    preferred_element_type=jnp.float32,
                ),
            ],
            axis=1,
        ),
        "tm",
        scatter_dimension=0,
        tiled=True,
    )
    grad_attn = lax.psum(row_share.astype(jnp.bfloat16), "batch").astype(jnp.float32)
    norm_correction_terms = jnp.stack(
        [
            jnp.sum(normalized_gradient * standardized_input, axis=0),
            jnp.sum(normalized_gradient, axis=0),
        ]
    )
    ln_grads = lax.psum(norm_correction_terms, ("tm", "batch"))
    gain_scaled_gradient = normalized_gradient * attention_norm_gain
    input_gradient = incoming_gradient.astype(jnp.float32) + inverse_deviation * (
        gain_scaled_gradient
        - jnp.mean(gain_scaled_gradient, axis=1, keepdims=True)
        - standardized_input
        * jnp.mean(gain_scaled_gradient * standardized_input, axis=1, keepdims=True)
    )
    grad_stem = (input_gradient * gelu_slope).astype(jnp.bfloat16)
    return (grad_stem[None], grad_attn, ln_grads)


def solution(mesh):
    placed = (
        P("batch", "tm", None),
        P(),
        P(),
        P(),
        P("batch", "tm", None),
        P("batch", "tm", None),
        P("batch", "tm", None),
        P("batch", "tm", None),
        P("batch", None),
    )
    return jax.shard_map(
        local,
        mesh=mesh,
        in_specs=placed,
        out_specs=(P("batch", "tm", None), P("tm", None), P()),
        check_vma=False,
    )
```

profile of v0, /device:TPU:1, one launch (start us, length us, event | category | flops | bytes accessed | tf_op | source)
XLA Modules:
  0.0 1135.2 jit_solution(5486297420431628950)
XLA Ops:
  1.7 3.3 collective-permute-start
  7.7 15.9 %collective-permute-done.1 = bf16[256,1280]{1,0:T(8,128)(2,1)S(1)} collective-permute-done((bf16[256,1280]{1,0:T(8,128)(2,1)S(1)}, bf16[256,1280]{1,0:T(8,128)(2,1)S(1)}, u32[]{:S(2)}, u32[]{:S(2)}) %collective-permute-start.1) | collective-permute-done | bytes 655392 | tf_op jit(solution)/shard_map/ppermute | solution.py:18
  25.2 28.2 %collective-permute-done.2 = bf16[512,1280]{1,0:T(8,128)(2,1)} collective-permute-done((bf16[512,1280]{1,0:T(8,128)(2,1)S(1)}, bf16[512,1280]{1,0:T(8,128)(2,1)}, u32[]{:S(2)}, u32[]{:S(2)}) %collective-permute-start.2) | collective-permute-done | bytes 1310752 | tf_op jit(solution)/shard_map/ppermute | solution.py:18
  53.4 2.9 maximum_select_fusion.1
  61.5 110.5 %collective-permute-done.3 = bf16[1024,1280]{1,0:T(8,128)(2,1)} collective-permute-done((bf16[1024,1280]{1,0:T(8,128)(2,1)S(1)}, bf16[1024,1280]{1,0:T(8,128)(2,1)}, u32[]{:S(2)}, u32[]{:S(2)}) %collective-permute-start.3) | collective-permute-done | bytes 2621472 | tf_op jit(solution)/shard_map/ppermute | solution.py:18
  172.0 3.3 maximum_select_fusion
  180.0 3.0 copy.34
  183.0 2.9 bitcast_reduce_fusion
  185.8 2.9 fusion.1
  188.8 3.1 fusion.33
  191.9 3.7 fusion.22
  195.6 4.8 multiply_convert_fusion
  205.6 115.3 %collective-permute-done.4 = bf16[1024,1280]{0,1:T(8,128)(2,1)S(1)} collective-permute-done((bf16[1024,1280]{0,1:T(8,128)(2,1)S(1)}, bf16[1024,1280]{0,1:T(8,128)(2,1)S(1)}, u32[]{:S(2)}, u32[]{:S(2)}) %collective-permute-start.4) | collective-permute-done | bytes 2621472 | tf_op jit(solution)/shard_map/ppermute | solution.py:18
  321.0 3.8 convert_add_fusion
  324.8 3.8 select_convert_fusion.1
  329.9 28.3 %collective-permute-done.5 = bf16[512,1280]{0,1:T(8,128)(2,1)} collective-permute-done((bf16[512,1280]{0,1:T(8,128)(2,1)}, bf16[512,1280]{0,1:T(8,128)(2,1)}, u32[]{:S(2)}, u32[]{:S(2)}) %collective-permute-start.5) | collective-permute-done | bytes 1310752 | tf_op jit(solution)/shard_map/ppermute | solution.py:18
  358.2 5.2 convert_add_fusion.1
  367.9 12.8 %collective-permute-done.6 = bf16[256,1280]{0,1:T(8,128)(2,1)} collective-permute-done((bf16[256,1280]{0,1:T(8,128)(2,1)}, bf16[256,1280]{0,1:T(8,128)(2,1)}, u32[]{:S(2)}, u32[]{:S(2)}) %collective-permute-start.6) | collective-permute-done | bytes 655392 | tf_op jit(solution)/shard_map/ppermute | solution.py:18
  383.1 2.9 collective-permute-start.7
  386.0 3.5 convolution_convert_fusion
  393.1 79.3 %psum.15 = f32[2,1280]{1,0:T(2,128)} all-reduce(f32[2,1280]{1,0:T(2,128)S(1)} %pad_maximum_fusion.6), channel_id=1, replica_groups=mesh['tm'=128,'batch'=2] {'tm','batch'}, use_global_device_ids=true, to_apply=%region_11.12 | all-reduce | flops 2560 | bytes 20480 | tf_op jit(solution)/shard_map/psum | solution.py:177
  475.2 5.3 pad_maximum_fusion
  480.5 643.3 %all-reduce.2 = bf16[1280,2560]{1,0:T(8,128)(2,1)} all-reduce(f32[1280,2560]{1,0:T(8,128)} %pad_maximum_fusion), channel_id=2, replica_groups=mesh['tm'=128,'batch'=2] {'tm'}, use_global_device_ids=true, to_apply=%region_7.8.clone | all-reduce | flops 3276800 | bytes 19660800
  1124.7 8.5 psum.14
  (87 shorter events, 36.9 us)
Async XLA Ops:
  0.6 57.4 %copy-start.14 = (bf16[1,128,640]{2,1,0:T(8,128)(2,1)S(1)}, bf16[1,128,640]{2,1,0:T(8,128)(2,1)}, u32[]{:S(2)}) copy-start(bf16[1,128,640]{2,1,0:T(8,128)(2,1)} %param.13) | copy-start | bytes 491524
  0.6 57.5 %copy-start.7 = (bf16[1,128,1280]{2,1,0:T(8,128)(2,1)S(1)}, bf16[1,128,1280]{2,1,0:T(8,128)(2,1)}, u32[]{:S(2)}) copy-start(bf16[1,128,1280]{2,1,0:T(8,128)(2,1)} %param.16) | copy-start | bytes 983044
  1.7 4.6 collective-permute-start
  7.6 16.0 %collective-permute-start.1 = (bf16[256,1280]{1,0:T(8,128)(2,1)S(1)}, bf16[256,1280]{1,0:T(8,128)(2,1)S(1)}, u32[]{:S(2)}, u32[]{:S(2)}) collective-permute-start(bf16[256,1280]{1,0:T(8,128)(2,1)S(1)} %maximum_select_fusion.3), channel_id=1, source_target_pairs={{0,4},{2,6},{4,0},{6,2},{8,12},{10,14},{12,8},{14,10},{16,20},{18,... | collective-permute-start | bytes 1966088 | tf_op jit(solution)/shard_map/ppermute | solution.py:18
  7.7 52.5 %copy-start.17 = (s32[1,8]{1,0:T(1,128)S(1)}, s32[1,8]{1,0:T(1,128)}, u32[]{:S(2)}) copy-start(s32[1,8]{1,0:T(1,128)} %param.17) | copy-start | bytes 100
  24.2 29.3 %collective-permute-start.2 = (bf16[512,1280]{1,0:T(8,128)(2,1)S(1)}, bf16[512,1280]{1,0:T(8,128)(2,1)}, u32[]{:S(2)}, u32[]{:S(2)}) collective-permute-start(bf16[512,1280]{1,0:T(8,128)(2,1)S(1)} %maximum_select_fusion.2), channel_id=1, source_target_pairs={{0,8},{2,10},{4,12},{6,14},{8,0},{10,2},{12,4},{14,6},{16,24},{18,... | collective-permute-start | bytes 3932168 | tf_op jit(solution)/shard_map/ppermute | solution.py:18
  56.3 115.7 %collective-permute-start.3 = (bf16[1024,1280]{1,0:T(8,128)(2,1)S(1)}, bf16[1024,1280]{1,0:T(8,128)(2,1)}, u32[]{:S(2)}, u32[]{:S(2)}) collective-permute-start(bf16[1024,1280]{1,0:T(8,128)(2,1)S(1)} %maximum_select_fusion.1), channel_id=1, source_target_pairs={{0,16},{2,18},{4,20},{6,22},{8,24},{10,26},{12,28},{14,30},{16,0},... | collective-permute-start | bytes 7864328 | tf_op jit(solution)/shard_map/ppermute | solution.py:18
  188.8 3.1 copy-start.5
  205.5 115.4 %collective-permute-start.4 = (bf16[1024,1280]{0,1:T(8,128)(2,1)S(1)}, bf16[1024,1280]{0,1:T(8,128)(2,1)S(1)}, u32[]{:S(2)}, u32[]{:S(2)}) collective-permute-start(bf16[1024,1280]{0,1:T(8,128)(2,1)S(1)} %select_convert_fusion), channel_id=1, source_target_pairs={{0,16},{2,18},{4,20},{6,22},{8,24},{10,26},{12,28},{14,30},{16,0},... | collective-permute-start | bytes 7864328 | tf_op jit(solution)/shard_map/ppermute | solution.py:18
  328.6 29.6 %collective-permute-start.5 = (bf16[512,1280]{0,1:T(8,128)(2,1)}, bf16[512,1280]{0,1:T(8,128)(2,1)}, u32[]{:S(2)}, u32[]{:S(2)}) collective-permute-start(bf16[512,1280]{0,1:T(8,128)(2,1)} %select_convert_fusion.1), channel_id=1, source_target_pairs={{0,8},{2,10},{4,12},{6,14},{8,0},{10,2},{12,4},{14,6},{16,24},{18,... | collective-permute-start | bytes 3932168 | tf_op jit(solution)/shard_map/ppermute | solution.py:18
  329.9 36.2 %copy-start.10 = (bf16[1,128,1280]{2,1,0:T(8,128)(2,1)S(1)}, bf16[1,128,1280]{2,1,0:T(8,128)(2,1)}, u32[]{:S(2)}) copy-start(bf16[1,128,1280]{2,1,0:T(8,128)(2,1)} %param.9) | copy-start | bytes 983044
  329.9 36.5 %copy-start.18 = (u32[256]{0:T(256)S(1)}, u32[256]{0:T(256)}, u32[]{:S(2)}) copy-start(u32[256]{0:T(256)} %constant.82) | copy-start | bytes 3076
  366.1 14.6 %collective-permute-start.6 = (bf16[256,1280]{0,1:T(8,128)(2,1)}, bf16[256,1280]{0,1:T(8,128)(2,1)}, u32[]{:S(2)}, u32[]{:S(2)}) collective-permute-start(bf16[256,1280]{0,1:T(8,128)(2,1)} %select_convert_fusion.2), channel_id=1, source_target_pairs={{0,4},{2,6},{4,0},{6,2},{8,12},{10,14},{12,8},{14,10},{16,20},{18,... | collective-permute-start | bytes 1966088 | tf_op jit(solution)/shard_map/ppermute | solution.py:18
  366.3 23.2 %copy-start.1 = (f32[128,1280]{1,0:T(8,128)}, f32[128,1280]{1,0:T(8,128)S(1)}, u32[]{:S(2)}) copy-start(f32[128,1280]{1,0:T(8,128)S(1)} %get-tuple-element.8) | copy-start | bytes 1966084
  380.7 9.7 slice-start
  383.0 6.5 copy-start.8
  383.0 6.5 copy-start.13
  383.1 7.3 slice-start.1
  383.1 7.2 collective-permute-start.7
  390.2 82.2 %copy-start.16 = (f32[1280]{0:T(1024)S(1)}, f32[1280]{0:T(1024)}, u32[]{:S(2)}) copy-start(f32[1280]{0:T(1024)} %param.11) | copy-start | bytes 15364
  480.4 653.4 %copy-start.3 = (f32[128,1280]{1,0:T(8,128)S(1)}, f32[128,1280]{1,0:T(8,128)}, u32[]{:S(2)}) copy-start(f32[128,1280]{1,0:T(8,128)} %copy-done.1) | copy-start | bytes 1966084
  480.4 653.4 %copy-start.9 = (bf16[1,128,1280]{2,1,0:T(8,128)(2,1)S(1)}, bf16[1,128,1280]{2,1,0:T(8,128)(2,1)}, u32[]{:S(2)}) copy-start(bf16[1,128,1280]{2,1,0:T(8,128)(2,1)} %param.16) | copy-start | bytes 983044
  480.4 653.4 %copy-start.11 = (bf16[1,128,1280]{2,1,0:T(8,128)(2,1)S(1)}, bf16[1,128,1280]{2,1,0:T(8,128)(2,1)}, u32[]{:S(2)}) copy-start(bf16[1,128,1280]{2,1,0:T(8,128)(2,1)} %param.9) | copy-start | bytes 983044
  480.4 653.4 %copy-start.12 = (f32[128,1280]{1,0:T(8,128)S(1)}, f32[128,1280]{1,0:T(8,128)}, u32[]{:S(2)}) copy-start(f32[128,1280]{1,0:T(8,128)} %get-tuple-element.17) | copy-start | bytes 1966084
  (5 other events, 8.0 us)
where the time goes:
time: 1140 us
  blocking collectives  731 us (64%)
  waiting for transfers between devices  312 us (27%)
  other arithmetic  42.9 us (4%)
  matrix products  27.5 us (2%)
    unnamed x1, blocking collectives  643 us
    ppermute x8, waiting for transfers between devices, swapped(): lax.ppermute(array, axis, [(i, i ^ 1 << stride) for i in range(lax.axis_s...  312 us
    psum x1, blocking collectives, local(): ln_grads = lax.psum(norm_correction_terms, ('tm', 'batch'))  79.3 us
  transfers between devices with their start and end apart: 8, of which 7 were waited for; matrix products, arithmetic and copies ran while one was open for 1% of the time, Pallas kernels for 0%

commit v1 on v0

v1 whole, which is shorter than its diff:
```python
import math

import jax
import jax.numpy as jnp
from jax import lax
from jax.experimental import pallas as pl
from jax.experimental.pallas import tpu as pltpu
from jax.sharding import PartitionSpec as P

HEAD_DIM = 64
HEADS = 10
SPAN = 16


NEG_FILL = -1e30
EPSILON = 1e-05


def gelu_and_slope(stem_in):
    normal_cdf = 0.5 * (1.0 + lax.erf(stem_in / math.sqrt(2.0)))
    density = jnp.exp(-0.5 * stem_in * stem_in) / math.sqrt(2.0 * math.pi)
    return (stem_in * normal_cdf, normal_cdf + stem_in * density)


def sinusoid(positions, features):
    half_width = features // 2
    frequency = jnp.exp(
        -math.log(10000.0) / (half_width - 1) * jnp.arange(half_width, dtype=jnp.float32)
    )
    angles = positions[:, None] * frequency[None, :]
    return jnp.concatenate([jnp.sin(angles), jnp.cos(angles)], axis=1)


OWNERS = (0, 2, 4, 5, 6, 8, 10, 11, 12, 14)
MESH = pl.DeviceIdType.MESH
ROWS = 128
BLOCK = 256


def attention_kernel(
    q_ref, k_ref, v_ref, go_ref, w_ref, frames_ref, out_ref,
    kv_out, qd_out, kv_in, qd_in, ret_qo, ret_kv, got, masked_k, kv_t, total,
    send_kv, send_qd, send_qo, send_dkv, recv_kv, recv_qd, recv_got,
):
    me = lax.axis_index("tm")
    slot = lax.rem(me, SPAN)
    base = me - slot

    barrier = pltpu.get_barrier_semaphore()
    for other in range(1, SPAN):
        peer = base + lax.rem(slot + other, SPAN)
        pl.semaphore_signal(barrier, inc=1, device_id={"tm": peer}, device_id_type=MESH)

    for h in range(HEADS):
        cols = slice(h * HEAD_DIM, (h + 1) * HEAD_DIM)
        kv_out[h] = jnp.concatenate([k_ref[0, :, cols], v_ref[0, :, cols]], axis=1)
    pl.semaphore_wait(barrier, SPAN - 1)

    def to_owner(h, buf, landing, send_sem, recv_sem):
        return pltpu.make_async_remote_copy(
            src_ref=buf.at[h], dst_ref=landing.at[slot],
            send_sem=send_sem.at[h], recv_sem=recv_sem,
            device_id={"tm": base + OWNERS[h]}, device_id_type=MESH,
        )

    def send_heads(buf, landing, send_sem, recv_sem):
        for h in range(HEADS):
            @pl.when(slot != OWNERS[h])
            def _():
                to_owner(h, buf, landing, send_sem, recv_sem).start()

            @pl.when(slot == OWNERS[h])
            def _():
                pltpu.make_async_copy(buf.at[h], landing.at[slot], recv_sem).start()

    send_heads(kv_out, kv_in, send_kv, recv_kv)
    grad_heads = jnp.dot(go_ref[0], w_ref[...], preferred_element_type=jnp.float32).astype(jnp.bfloat16)
    for h in range(HEADS):
        cols = slice(h * HEAD_DIM, (h + 1) * HEAD_DIM)
        qd_out[h] = jnp.concatenate([q_ref[0, :, cols], grad_heads[:, cols]], axis=1)
    send_heads(qd_out, qd_in, send_qd, recv_qd)

    head = jnp.int32(0)
    active = jnp.bool_(False)
    for h in range(HEADS):
        head = jnp.where(slot == OWNERS[h], h, head)
        active = jnp.logical_or(active, slot == OWNERS[h])
    seq = SPAN * ROWS

    def back(buf, index, part, send_sem):
        return pltpu.make_async_remote_copy(
            src_ref=buf.at[index], dst_ref=got.at[part, head],
            send_sem=send_sem.at[index], recv_sem=recv_got,
            device_id={"tm": base + index}, device_id_type=MESH,
        )

    def send_back(buf, index, part, send_sem):
        @pl.when(slot != index)
        def _():
            back(buf, index, part, send_sem).start()

        @pl.when(slot == index)
        def _():
            pltpu.make_async_copy(buf.at[index], got.at[part, head], recv_got).start()

    @pl.when(active)
    def _():
        limit = frames_ref[0, me // SPAN]
        pltpu.make_async_copy(kv_in, kv_in, recv_kv).wait()
        kv = kv_in[...].reshape(seq, 2 * HEAD_DIM)
        lane = lax.broadcasted_iota(jnp.int32, kv.shape, 1)
        row = lax.broadcasted_iota(jnp.int32, kv.shape, 0)
        fill = jnp.where(jnp.logical_and(lane == HEAD_DIM, 2 * row >= limit), NEG_FILL, 0.0)
        masked_k[...] = jnp.where(lane < HEAD_DIM, kv.astype(jnp.float32), fill).astype(jnp.bfloat16)
        kv_t[...] = kv.T
        total[...] = jnp.zeros_like(total)
        pltpu.make_async_copy(qd_in, qd_in, recv_qd).wait()
        scale = 1.0 / math.sqrt(HEAD_DIM)
        blane = lax.broadcasted_iota(jnp.int32, (BLOCK, 2 * HEAD_DIM), 1)
        brow = lax.broadcasted_iota(jnp.int32, (2 * HEAD_DIM, BLOCK), 0)

        def body(i, carry):
            qd = qd_in[pl.ds(2 * i, 2)].reshape(BLOCK, 2 * HEAD_DIM).astype(jnp.float32)
            q_ones = jnp.where(blane < HEAD_DIM, qd * scale, jnp.where(blane == HEAD_DIM, 1.0, 0.0)).astype(jnp.bfloat16)
            q_only = jnp.where(blane < HEAD_DIM, qd, 0.0).astype(jnp.bfloat16)
            d_only = jnp.where(blane >= HEAD_DIM, qd, 0.0).astype(jnp.bfloat16)
            scores = lax.dot_general(
                masked_k[...], q_ones, (((1,), (1,)), ((), ())), preferred_element_type=jnp.float32
            )
            top = jnp.max(scores, axis=0, keepdims=True)
            power = jnp.exp(scores - top)
            prob = power * (1.0 / jnp.sum(power, axis=0, keepdims=True))
            prob_b = prob.astype(jnp.bfloat16)
            attn_t = jnp.dot(kv_t[...], prob_b, preferred_element_type=jnp.float32)
            attn_t = attn_t.astype(jnp.bfloat16).astype(jnp.float32)
            delta = jnp.sum(jnp.where(brow >= HEAD_DIM, qd.T * attn_t, 0.0), axis=0, keepdims=True)
            grad_prob = lax.dot_general(
                kv_in[...].reshape(seq, 2 * HEAD_DIM), d_only, (((1,), (1,)), ((), ())), preferred_element_type=jnp.float32
            )
            dscore = (prob * (grad_prob - delta) * scale).astype(jnp.bfloat16)
            dq_t = jnp.dot(kv_t[...], dscore, preferred_element_type=jnp.float32)
            result = jnp.where(brow < HEAD_DIM, dq_t, attn_t).T.astype(jnp.bfloat16)
            ret_qo[pl.ds(2 * i, 2)] = result.reshape(2, ROWS, 2 * HEAD_DIM)
            send_back(ret_qo, 2 * i, 0, send_qo)
            send_back(ret_qo, 2 * i + 1, 0, send_qo)
            total[...] += jnp.dot(dscore, q_only, preferred_element_type=jnp.float32) + jnp.dot(
                prob_b, d_only, preferred_element_type=jnp.float32
            )
            return carry

        lax.fori_loop(0, seq // BLOCK, body, 0)
        ret_kv[...] = total[...].astype(jnp.bfloat16).reshape(SPAN, ROWS, 2 * HEAD_DIM)

        def send_kv_grads(i, carry):
            send_back(ret_kv, i, 1, send_dkv)
            return carry

        lax.fori_loop(0, SPAN, send_kv_grads, 0)

    pltpu.make_async_copy(got, got, recv_got).wait()
    for h in range(HEADS):
        for part, (left, right) in enumerate(((0, 3), (1, 2))):
            tile = got[part, h]
            out_ref[:, left * HEADS * HEAD_DIM + h * HEAD_DIM : left * HEADS * HEAD_DIM + (h + 1) * HEAD_DIM] = tile[:, :HEAD_DIM]
            out_ref[:, right * HEADS * HEAD_DIM + h * HEAD_DIM : right * HEADS * HEAD_DIM + (h + 1) * HEAD_DIM] = tile[:, HEAD_DIM:]

    for h in range(HEADS):
        @pl.when(slot != OWNERS[h])
        def _():
            to_owner(h, kv_out, kv_in, send_kv, recv_kv).wait_send()
            to_owner(h, qd_out, qd_in, send_qd, recv_qd).wait_send()

    @pl.when(active)
    def _():
        def drain(i, carry):
            @pl.when(slot != i)
            def _():
                back(ret_qo, i, 0, send_qo).wait_send()
                back(ret_kv, i, 1, send_dkv).wait_send()
            return carry

        lax.fori_loop(0, SPAN, drain, 0)


def attention_exchange(queries, keys, values, grad_out, w_attn, frames):
    width = HEADS * HEAD_DIM
    rows, features = grad_out.shape[1:]
    tile = (ROWS, 2 * HEAD_DIM)
    seq = SPAN * ROWS
    vmem = pltpu.VMEM
    return pl.pallas_call(
        attention_kernel,
        grid=(1,),
        out_shape=jax.ShapeDtypeStruct((rows, 4 * width), jnp.bfloat16),
        in_specs=[
            pl.BlockSpec((1, rows, width), lambda i: (0, 0, 0)),
            pl.BlockSpec((1, rows, width), lambda i: (0, 0, 0)),
            pl.BlockSpec((1, rows, width), lambda i: (0, 0, 0)),
            pl.BlockSpec((1, rows, features), lambda i: (0, 0, 0)),
            pl.BlockSpec((features, width), lambda i: (0, 3)),
            pl.BlockSpec(memory_space=pltpu.SMEM),
        ],
        out_specs=pl.BlockSpec((rows, 4 * width), lambda i: (0, 0)),
        scratch_shapes=[
            vmem((HEADS,) + tile, jnp.bfloat16),
            vmem((HEADS,) + tile, jnp.bfloat16),
            vmem((SPAN,) + tile, jnp.bfloat16),
            vmem((SPAN,) + tile, jnp.bfloat16),
            vmem((SPAN,) + tile, jnp.bfloat16),
            vmem((SPAN,) + tile, jnp.bfloat16),
            vmem((2, HEADS) + tile, jnp.bfloat16),
            vmem((seq, 2 * HEAD_DIM), jnp.bfloat16),
            vmem((2 * HEAD_DIM, seq), jnp.bfloat16),
            vmem((seq, 2 * HEAD_DIM), jnp.float32),
            pltpu.SemaphoreType.DMA((HEADS,)),
            pltpu.SemaphoreType.DMA((HEADS,)),
            pltpu.SemaphoreType.DMA((SPAN,)),
            pltpu.SemaphoreType.DMA((SPAN,)),
            pltpu.SemaphoreType.DMA,
            pltpu.SemaphoreType.DMA,
            pltpu.SemaphoreType.DMA,
        ],
        compiler_params=pltpu.CompilerParams(
            collective_id=0, has_side_effects=True, vmem_limit_bytes=50 * 1024 * 1024
        ),
        name="attention_exchange",
    )(queries, keys, values, grad_out, w_attn, frames)


N_X, N_Z, QUAD, N_Y = 4, 8, 4, 2
PIECE = 640
X_ROWS = 320
HALF = 160
Z_ROWS = 40
Z_PAD = 48
OUT_ROWS = 10
OUT_PAD = 16


def weight_kernel(
    normed_ref, go_ref, cols_ref, norm_ref, out_ref, norm_out_ref,
    left, right, wide, sends, first, joined, alone, joint_out, z_out, z_in, last_out, last_in,
    norm_a, norm_b, norm_c, norm_mid,
    s_left, s_right, s_first, s_joined, s_alone, s_z, s_last, s_na, s_nb, s_nc,
    r_left, r_right, r_first, r_joined, r_alone, r_z, r_last, r_na, r_nb, r_nc,
):
    me = lax.axis_index("tm")
    side = lax.axis_index("batch")
    t = lax.rem(me, QUAD)
    z = lax.rem(me // QUAD, N_Z)
    x = me // (QUAD * N_Z)
    mine8 = side * QUAD + t

    def at_x(step):
        return {"tm": lax.rem(x + step, N_X) * (QUAD * N_Z) + z * QUAD + t}

    def at_z(step):
        return {"tm": x * (QUAD * N_Z) + lax.rem(z + step, N_Z) * QUAD + t}

    def at_quad(step):
        return {"tm": x * (QUAD * N_Z) + z * QUAD + lax.rem(t + step, QUAD)}

    def at_eight(step):
        place = lax.rem(mine8 + step, 2 * QUAD)
        return {"tm": x * (QUAD * N_Z) + z * QUAD + lax.rem(place, QUAD), "batch": place // QUAD}

    def remote(src, dst, send_sem, recv_sem, device):
        return pltpu.make_async_remote_copy(
            src_ref=src, dst_ref=dst, send_sem=send_sem, recv_sem=recv_sem,
            device_id=device, device_id_type=MESH,
        )

    def landed(buf, sem):
        pltpu.make_async_copy(buf, buf, sem).wait()

    barrier = pltpu.get_barrier_semaphore()
    for step in range(1, N_X):
        pl.semaphore_signal(barrier, inc=1, device_id=at_x(step), device_id_type=MESH)
    for step in range(1, N_Z):
        pl.semaphore_signal(barrier, inc=1, device_id=at_z(step), device_id_type=MESH)
    for step in range(1, 2 * QUAD):
        pl.semaphore_signal(barrier, inc=1, device_id=at_eight(step), device_id_type=MESH)
    pl.semaphore_wait(barrier, N_X - 1 + N_Z - 1 + 2 * QUAD - 1)

    pending = []

    def go(copy):
        copy.start()
        pending.append(copy)

    for step in range(1, QUAD):
        other = lax.rem(t + step, QUAD)
        columns = pl.ds(pl.multiple_of(other * PIECE, 128), PIECE)
        go(remote(cols_ref.at[:, columns], right.at[t], s_right.at[step], r_right, at_quad(step)))
    own_columns = pl.ds(pl.multiple_of(t * PIECE, 128), PIECE)
    pltpu.make_async_copy(cols_ref.at[:, own_columns], right.at[t], r_right).start()
    for step in range(1, QUAD):
        other = lax.rem(t + step, QUAD)
        from_normed = remote(normed_ref, left.at[t], s_left.at[step], r_left, at_quad(step))
        from_go = remote(go_ref.at[0], left.at[t], s_left.at[step], r_left, at_quad(step))
        pl.when(other < QUAD - 1)(from_normed.start)
        pl.when(other == QUAD - 1)(from_go.start)
        pending.append(from_normed)
    pl.when(t < QUAD - 1)(pltpu.make_async_copy(normed_ref, left.at[t], r_left).start)
    pl.when(t == QUAD - 1)(pltpu.make_async_copy(go_ref.at[0], left.at[t], r_left).start)

    for step in range(1, N_Z):
        go(remote(norm_ref, norm_a.at[z], s_na.at[step], r_na, at_z(step)))
    pltpu.make_async_copy(norm_ref, norm_a.at[z], r_na).start()
    landed(norm_a, r_na)
    norm_mid[0] = jnp.sum(norm_a[...], axis=0)
    for step in range(1, N_X):
        go(remote(norm_mid.at[0], norm_b.at[x], s_nb.at[step], r_nb, at_x(step)))
    pltpu.make_async_copy(norm_mid.at[0], norm_b.at[x], r_nb).start()
    landed(norm_b, r_nb)
    norm_mid[1] = jnp.sum(norm_b[...], axis=0)
    for step in range(1, 2 * QUAD):
        go(remote(norm_mid.at[1], norm_c.at[mine8], s_nc.at[step], r_nc, at_eight(step)))
    pltpu.make_async_copy(norm_mid.at[1], norm_c.at[mine8], r_nc).start()

    landed(right, r_right)
    landed(left, r_left)
    tokens = QUAD * ROWS
    features = N_X * X_ROWS
    for at in range(0, features, 256):
        product = lax.dot_general(
            left[:, :, at : at + 256].reshape(tokens, 256),
            right[...].reshape(tokens, PIECE),
            (((0,), (0,)), ((), ())),
            preferred_element_type=jnp.float32,
        )
        wide[at : at + 256] = product
        sends[at : at + 256] = product.astype(jnp.bfloat16)

    def rows_of(step, half):
        chunk = lax.rem(x + step, N_X)
        return pl.ds(pl.multiple_of(chunk * X_ROWS + half * HALF, 32), HALF)

    for half, step in ((0, 1), (1, N_X - 1)):
        go(remote(sends.at[rows_of(2, half)], first.at[half], s_first.at[half], r_first.at[half], at_x(step)))
    for half, step in ((0, 1), (1, N_X - 1)):
        go(remote(sends.at[rows_of(step, 1 - half)], alone.at[1 - half], s_alone.at[half], r_alone.at[1 - half], at_x(step)))
    for half, step in ((0, 1), (1, N_X - 1)):
        landed(first.at[half], r_first.at[half])
        joint_out[half] = (first[half].astype(jnp.float32) + wide[rows_of(step, half)]).astype(jnp.bfloat16)
        go(remote(joint_out.at[half], joined.at[half], s_joined.at[half], r_joined.at[half], at_x(step)))

    for half in range(2):
        landed(alone.at[half], r_alone.at[half])
        landed(joined.at[half], r_joined.at[half])
        total = wide[rows_of(0, half)] + alone[half].astype(jnp.float32) + joined[half].astype(jnp.float32)
        for part in range(HALF // Z_ROWS):
            z_out[half * (HALF // Z_ROWS) + part] = jnp.concatenate(
                [total[part * Z_ROWS : (part + 1) * Z_ROWS], jnp.zeros((Z_PAD - Z_ROWS, PIECE), jnp.float32)], axis=0
            ).astype(jnp.bfloat16)
    for step in range(1, N_Z):
        go(remote(z_out.at[lax.rem(z + step, N_Z)], z_in.at[z], s_z.at[step], r_z, at_z(step)))
    pltpu.make_async_copy(z_out.at[z], z_in.at[z], r_z).start()
    landed(norm_c, r_nc)
    norm_out_ref[...] = jnp.sum(norm_c[...], axis=0)
    landed(z_in, r_z)
    total = jnp.sum(z_in[...].astype(jnp.float32), axis=0)[:Z_ROWS]

    for place in range(QUAD):
        last_out[place] = jnp.concatenate(
            [total[place * OUT_ROWS : (place + 1) * OUT_ROWS], jnp.zeros((OUT_PAD - OUT_ROWS, PIECE), jnp.float32)], axis=0
        )
    for step in range(1, 2 * QUAD):
        place = lax.rem(lax.rem(mine8 + step, 2 * QUAD), QUAD)
        go(remote(last_out.at[place], last_in.at[mine8], s_last.at[step], r_last, at_eight(step)))
    pltpu.make_async_copy(last_out.at[t], last_in.at[mine8], r_last).start()
    landed(last_in, r_last)
    for block in range(QUAD):
        both = last_in[block] + last_in[QUAD + block]
        out_ref[:, block * PIECE : (block + 1) * PIECE] = both[:OUT_ROWS]
    for copy in pending:
        copy.wait_send()


def weight_exchange(normed, grad_out, columns, norm_terms):
    rows, features = normed.shape
    vmem, dma = pltpu.VMEM, pltpu.SemaphoreType.DMA
    bf, f32 = jnp.bfloat16, jnp.float32
    return pl.pallas_call(
        weight_kernel,
        out_shape=(
            jax.ShapeDtypeStruct((OUT_ROWS, QUAD * PIECE), f32),
            jax.ShapeDtypeStruct(norm_terms.shape, f32),
        ),
        in_specs=[pl.BlockSpec(memory_space=vmem)] * 4,
        out_specs=(pl.BlockSpec(memory_space=vmem), pl.BlockSpec(memory_space=vmem)),
        scratch_shapes=[
            vmem((QUAD, rows, features), bf),
            vmem((QUAD, rows, PIECE), bf),
            vmem((features, PIECE), f32),
            vmem((features, PIECE), bf),
            vmem((2, HALF, PIECE), bf),
            vmem((2, HALF, PIECE), bf),
            vmem((2, HALF, PIECE), bf),
            vmem((2, HALF, PIECE), bf),
            vmem((N_Z, Z_PAD, PIECE), bf),
            vmem((N_Z, Z_PAD, PIECE), bf),
            vmem((QUAD, OUT_PAD, PIECE), f32),
            vmem((2 * QUAD, OUT_PAD, PIECE), f32),
            vmem((N_Z,) + norm_terms.shape, f32),
            vmem((N_X,) + norm_terms.shape, f32),
            vmem((2 * QUAD,) + norm_terms.shape, f32),
            vmem((2,) + norm_terms.shape, f32),
            dma((QUAD,)), dma((QUAD,)), dma((2,)), dma((2,)), dma((2,)),
            dma((N_Z,)), dma((2 * QUAD,)), dma((N_Z,)), dma((N_X,)), dma((2 * QUAD,)),
            dma, dma, dma((2,)), dma((2,)), dma((2,)), dma, dma, dma, dma, dma,
        ],
        compiler_params=pltpu.CompilerParams(
            collective_id=1, has_side_effects=True, vmem_limit_bytes=50 * 1024 * 1024
        ),
        name="weight_exchange",
    )(normed, grad_out, columns, norm_terms)


def local(
    stem_pre,
    attention_norm_gain,
    attention_norm_bias,
    w_attn,
    queries,
    keys,
    values,
    grad_out,
    frames,
):
    tok_rows = stem_pre.shape[1]
    features = stem_pre.shape[2]
    head_width = queries.shape[2]
    group_slot = lax.axis_index("tm") % SPAN
    offset = group_slot * tok_rows
    stem_in = stem_pre[0].astype(jnp.float32)
    activated, gelu_slope = gelu_and_slope(stem_in)
    positions = (offset + jnp.arange(tok_rows)).astype(jnp.float32)
    embedded = activated + sinusoid(positions, features)
    row_mean = jnp.mean(embedded, axis=1, keepdims=True)
    centered_input = embedded - row_mean
    inverse_deviation = lax.rsqrt(
        jnp.mean(centered_input * centered_input, axis=1, keepdims=True) + EPSILON
    )
    standardized_input = centered_input * inverse_deviation
    normalized_input = (standardized_input * attention_norm_gain + attention_norm_bias).astype(
        jnp.bfloat16
    )
    incoming_gradient = grad_out[0]
    columns = attention_exchange(queries, keys, values, grad_out, w_attn, frames)
    grad_qkv = columns[:, : 3 * head_width]
    normalized_gradient = lax.dot_general(
        grad_qkv,
        w_attn[:, : 3 * head_width],
        (((1,), (1,)), ((), ())),
        preferred_element_type=jnp.float32,
    )
    norm_terms = jnp.stack(
        [
            jnp.sum(normalized_gradient * standardized_input, axis=0),
            jnp.sum(normalized_gradient, axis=0),
        ]
    )
    packed = jnp.pad(norm_terms.reshape(-1, ROWS), ((0, 4), (0, 0)))
    grad_attn, norm_sums = weight_exchange(normalized_input, grad_out, columns, packed)
    ln_grads = norm_sums[: 2 * features // ROWS].reshape(2, features)
    gain_scaled_gradient = normalized_gradient * attention_norm_gain
    input_gradient = incoming_gradient.astype(jnp.float32) + inverse_deviation * (
        gain_scaled_gradient
        - jnp.mean(gain_scaled_gradient, axis=1, keepdims=True)
        - standardized_input
        * jnp.mean(gain_scaled_gradient * standardized_input, axis=1, keepdims=True)
    )
    grad_stem = (input_gradient * gelu_slope).astype(jnp.bfloat16)
    return (grad_stem[None], grad_attn, ln_grads)


def solution(mesh):
    placed = (
        P("batch", "tm", None),
        P(),
        P(),
        P(),
        P("batch", "tm", None),
        P("batch", "tm", None),
        P("batch", "tm", None),
        P("batch", "tm", None),
        P("batch", None),
    )
    return jax.shard_map(
        local,
        mesh=mesh,
        in_specs=placed,
        out_specs=(P("batch", "tm", None), P("tm", None), P()),
        check_vma=False,
    )
```

time: 1140 us -> 128 us (0.11)
  blocking collectives: 731 us -> 0 us
  waiting for transfers between devices: 312 us -> 0 us
  Pallas kernels: 0 us -> 116 us
  other arithmetic: 42.9 us -> 4.01 us
  matrix products: 27.5 us -> 1.63 us
    unnamed x1 -> x0, blocking collectives: 643 us -> none
    ppermute x8 -> x0, waiting for transfers between devices: 312 us -> none  [swapped(): lax.ppermute(array, axis, [(i, i ^ 1 << stride) for i in range(lax.axis_s...]
    pallas_call x0 -> x2, Pallas kernels: none -> 116 us  [the longest x1 59.7 us: weight_exchange(): pl.pallas_call(weight_kernel, out_shape=(jax.ShapeDtypeStruct((OUT_ROWS,...]
    psum x2 -> x0, blocking collectives: 87.8 us -> none  [the longest x1 79.3 us: local(): ln_grads = lax.psum(norm_correction_terms, ('tm', 'batch'))]
    dot_general x9 -> x0, matrix products: 25.2 us -> none  [the longest x1 4.8 us: local(): jnp.einsum('qhd,khd->hqk', cot_heads, value_heads, preferred_element_type...]
  transfers between devices with their start and end apart: 8 -> 0, of which waited for: 7 -> 0; matrix products, arithmetic and copies ran while one was open for 1% -> 0% of each run, Pallas kernels for 0% -> 0%
where the time goes in v1:
time: 128 us
  Pallas kernels  116 us (91%)
  local copies, waits for them, and re-layouts  5.71 us (4%)
  other arithmetic  4.01 us (3%)
  matrix products  1.63 us (1%)
    pallas_call x1, Pallas kernels, weight_exchange(): pl.pallas_call(weight_kernel, out_shape=(jax.ShapeDtypeStruct((OUT_ROWS,...  59.7 us
    pallas_call x1, Pallas kernels, attention_exchange(): pl.pallas_call(attention_kernel, grid=(1,), out_shape=jax.ShapeDtypeStruc...  56.2 us
    unnamed x21, local copies, waits for them, and re-layouts  5.07 us

profile of v1, /device:TPU:1, one launch (start us, length us, event | category | flops | bytes accessed | tf_op | source)
XLA Modules:
  0.0 128.0 jit_solution(17779281108124267448)
XLA Ops:
  0.6 0.0 copy-start.8
  0.6 0.0 copy-start.9
  0.7 1.2 multiply_sine_fusion
  1.9 1.2 fusion.13
  3.1 0.2 multiply_reduce_fusion.2
  3.4 0.0 copy-start
  3.4 1.0 copy-done
  4.4 0.9 copy-done.2
  5.3 0.9 copy-done.3
  6.2 0.9 copy-done.4
  7.1 0.7 copy-done.5
  7.8 56.2 %attention_exchange.1.cols_ref = bf16[128,2560]{1,0:T(8,128)(2,1)S(1)} custom-call(bf16[1,128,640]{2,1,0:T(8,128)(2,1)S(1)} %copy-done.2, bf16[1,128,640]{2,1,0:T(8,128)(2,1)S(1)} %copy-done.3, bf16[1,128,640]{2,1,0:T(8,128)(2,1)S(1)} %copy-done.4, bf16[1,128,1280]{2,1,0:T(8,128)(2,1)S(1)} %copy-done, bf16[1280,2560]{1,0:T(8,128)(2,1)} %w_ref.1, ...), custom_call_target="tpu_custom_call" | custom-call | tf_op jit(solution)/shard_map/attention_exchange/pallas_call | solution.py:191
  64.0 0.0 copy-done.8
  64.0 0.0 copy-done.9
  64.0 0.0 copy-done.6
  64.0 0.0 copy-start.1
  64.0 0.0 copy-start.7
  64.0 1.6 %multiply_reduce_fusion = (f32[1280]{0:T(1024)S(1)}, f32[128]{0:T(128)S(1)}, f32[128]{0:T(128)S(1)}, f32[1280]{0:T(1024)S(1)}, bf16[128,1280]{1,0:T(8,128)(2,1)S(1)}, /*index=5*/f32[128,1280]{1,0:T(8,128)S(1)}) fusion(f32[128,1280]{1,0:T(8,128)S(1)} %get-tuple-element.12, f32[128]{0:T(128)S(1)} %add_rsqrt_fusion, f32[128]{0:T(128)S(1)} %broadcast_multiply_fusion.2, ...), kind=kOutput, calls=%fused_computation.17 | convolution fusion | flops 631108864 | bytes 7073792 | tf_op jit(solution)/shard_map/dot_general | solution.py:452
  65.7 0.0 copy-done.1
  65.7 59.7 %weight_exchange.1 = (f32[10,2560]{1,0:T(8,128)S(1)}, f32[24,128]{1,0:T(8,128)S(1)}) custom-call(bf16[128,1280]{1,0:T(8,128)(2,1)S(1)} %get-tuple-element.13.normed_ref, bf16[1,128,1280]{2,1,0:T(8,128)(2,1)S(1)} %copy-done.1, bf16[128,2560]{1,0:T(8,128)(2,1)S(1)} %attention_exchange.1.cols_ref, f32[24,128]{1,0:T(8,128)S(1)} %pad.4.norm_ref), custom_call_target="tpu_custom_call" | custom-call | tf_op jit(solution)/shard_map/weight_exchange/pallas_call | solution.py:384
  125.5 0.6 reshape.49
  126.1 0.0 copy-done.7
  126.1 1.3 %fusion.12 = bf16[1,128,1280]{2,1,0:T(8,128)(2,1)} fusion(bf16[1,128,1280]{2,1,0:T(8,128)(2,1)S(1)} %copy-done.7, f32[128]{0:T(128)S(1)} %get-tuple-element.17, f32[128,1280]{1,0:T(8,128)S(1)} %get-tuple-element.12, f32[128]{0:T(128)S(1)} %broadcast_multiply_fusion.2, f32[128]{0:T(128)S(1)} %get-tuple-element.18, f32[128,1280]{1,0:T(8,128)S(1)} %get-tuple-element.16, ...), kind=kLoop, calls=%fused_computation.26 | loop fusion | flops 3276800 | bytes 2300928 | tf_op jit(solution)/shard_map/broadcast_in_dim | solution.py:475
  127.4 0.7 copy.13
  (15 shorter events, 0.1 us)
Async XLA Ops:
  0.6 63.3 %copy-start.8 = (f32[1280]{0:T(1024)S(1)}, f32[1280]{0:T(1024)}, u32[]{:S(2)}) copy-start(f32[1280]{0:T(1024)} %param.10) | copy-start | bytes 15364
  0.6 63.3 %copy-start.9 = (f32[1280]{0:T(1024)S(1)}, f32[1280]{0:T(1024)}, u32[]{:S(2)}) copy-start(f32[1280]{0:T(1024)} %param.11) | copy-start | bytes 15364
  3.4 1.0 copy-start
  4.4 0.9 copy-start.2
  5.3 0.9 copy-start.3
  6.2 0.9 copy-start.4
  7.1 0.7 copy-start.5
  7.8 56.2 %copy-start.6 = (bf16[1280,2560]{1,0:T(8,128)(2,1)S(1)}, bf16[1280,2560]{1,0:T(8,128)(2,1)}, u32[]{:S(2)}) copy-start(bf16[1280,2560]{1,0:T(8,128)(2,1)} %w_ref.1) | copy-start | bytes 19660804
  64.0 1.7 %copy-start.1 = (bf16[1,128,1280]{2,1,0:T(8,128)(2,1)S(1)}, bf16[1,128,1280]{2,1,0:T(8,128)(2,1)}, u32[]{:S(2)}) copy-start(bf16[1,128,1280]{2,1,0:T(8,128)(2,1)} %go_ref.3) | copy-start | bytes 983044
  64.0 62.1 %copy-start.7 = (bf16[1,128,1280]{2,1,0:T(8,128)(2,1)S(1)}, bf16[1,128,1280]{2,1,0:T(8,128)(2,1)}, u32[]{:S(2)}) copy-start(bf16[1,128,1280]{2,1,0:T(8,128)(2,1)} %param.9) | copy-start | bytes 983044

commit v2 on v0

v2 whole, which is shorter than its diff:
```python
import math

import jax
import jax.numpy as jnp
from jax import lax
from jax.experimental import pallas as pl
from jax.experimental.pallas import tpu as pltpu
from jax.sharding import PartitionSpec as P

HEAD_DIM = 64
HEADS = 10
SPAN = 16
NEG_FILL = -1e30
EPSILON = 1e-05

OWNERS = (0, 4, 5, 8, 12, 2, 6, 10, 11, 14)
MESH = pl.DeviceIdType.MESH
D = 1280
WIDTH = HEADS * HEAD_DIM
PAIR = 2 * HEAD_DIM
GROUP = HEADS // 2
ROWS = 128
BLOCK = 256
SEQ = SPAN * ROWS
N_X, N_Z, QUAD = 4, 8, 4
PIECE = GROUP * PAIR
X_ROWS = 160
HALF = X_ROWS // 2
Z_ROWS = 40
Z_PAD = 48
OUT_ROWS = 10
OUT_PAD = 16
NORM_ROWS = 24
TILES = D // 128
BF, F32 = jnp.bfloat16, jnp.float32


def layer_kernel(
    stem_hbm, gain_ref, bias_ref, w_hbm, q_hbm, k_hbm, v_hbm, go_hbm, frames_ref,
    stem_out, out_ref, norm_out,
    stem_ref, w_out, w_qkv, q_ref, k_ref, v_ref, go_ref,
    kv_out, qd_out, kv_in, qd_in, ret_qo, ret_kv, masked_k, kv_t, total,
    xhat, slope, deviation, left_out, left_in, cols, tok_in,
    wide, sends, first, joined, alone, joint_out, z_out, z_in, last_out, last_in,
    norm_a, norm_b, norm_c, norm_mid,
    s_load, s_kv, s_qd, s_qo, s_dkv, s_left, s_pair, s_tok, s_first, s_joined, s_alone, s_z, s_last,
    s_na, s_nb, s_nc,
    r_kv, r_qd, r_cols, r_left, r_pair, r_tok, r_first, r_joined, r_alone, r_z, r_last, r_na, r_nb, r_nc,
):
    me = lax.axis_index("tm")
    side = lax.axis_index("batch")
    slot = lax.rem(me, SPAN)
    base = me - slot
    core = lax.rem(me, 2)
    low = lax.rem(me // 2, 2)
    t = lax.rem(me, QUAD)
    z = lax.rem(me // QUAD, N_Z)
    x = me // (QUAD * N_Z)
    mine8 = side * QUAD + t

    loads = {}
    for index, (name, src, dst) in enumerate(
        (
            ("k", k_hbm.at[0], k_ref), ("v", v_hbm.at[0], v_ref), ("q", q_hbm.at[0], q_ref), ("go", go_hbm.at[0], go_ref),
            ("w_out", w_hbm.at[:, pl.ds(3 * WIDTH, WIDTH)], w_out), ("stem", stem_hbm.at[0], stem_ref),
            ("w_qkv", w_hbm.at[:, pl.ds(0, 3 * WIDTH)], w_qkv),
        )
    ):
        loads[name] = pltpu.make_async_copy(src, dst, s_load.at[index])
        loads[name].start()

    def at_x(step):
        return {"tm": lax.rem(x + step, N_X) * (QUAD * N_Z) + z * QUAD + t}

    def at_z(place):
        return {"tm": x * (QUAD * N_Z) + place * QUAD + t}

    def at_quad(place):
        return {"tm": x * (QUAD * N_Z) + z * QUAD + place}

    def at_eight(step):
        place = lax.rem(mine8 + step, 2 * QUAD)
        return {"tm": x * (QUAD * N_Z) + z * QUAD + lax.rem(place, QUAD), "batch": place // QUAD}

    def remote(src, dst, send_sem, recv_sem, device):
        return pltpu.make_async_remote_copy(
            src_ref=src, dst_ref=dst, send_sem=send_sem, recv_sem=recv_sem,
            device_id=device, device_id_type=MESH,
        )

    def landed(buf, sem):
        pltpu.make_async_copy(buf, buf, sem).wait()

    barrier = pltpu.get_barrier_semaphore()

    def greet(device):
        pl.semaphore_signal(barrier, inc=1, device_id=device, device_id_type=MESH)

    for step in range(1, SPAN):
        greet({"tm": base + lax.rem(slot + step, SPAN)})
    for step in range(1, N_X):
        greet(at_x(step))
    for place in range(QUAD):
        greet(at_z((1 - z // QUAD) * QUAD + place))
    for place in range(QUAD):
        greet({"tm": x * (QUAD * N_Z) + z * QUAD + place, "batch": 1 - side})

    pending = []

    def go(copy):
        copy.start()
        pending.append(copy)

    def go_or_copy(here, copy, src, dst, recv_sem, keep=True):
        pl.when(jnp.logical_not(here))(copy.start)
        pl.when(here)(pltpu.make_async_copy(src, dst, recv_sem).start)
        if keep:
            pending.append((here, copy))

    loads["k"].wait()
    loads["v"].wait()
    for h in range(HEADS):
        at = slice(h * HEAD_DIM, (h + 1) * HEAD_DIM)
        kv_out[h] = jnp.concatenate([k_ref[:, at], v_ref[:, at]], axis=1)
    pl.semaphore_wait(barrier, SPAN - 1 + N_X - 1 + 2 * QUAD)
    for h in range(HEADS):
        copy = remote(kv_out.at[h], kv_in.at[slot], s_kv.at[h], r_kv, {"tm": base + OWNERS[h]})
        go_or_copy(slot == OWNERS[h], copy, kv_out.at[h], kv_in.at[slot], r_kv)
    loads["q"].wait()
    loads["go"].wait()
    loads["w_out"].wait()
    grad_heads = jnp.dot(go_ref[...], w_out[...], preferred_element_type=F32).astype(BF)
    for h in range(HEADS):
        at = slice(h * HEAD_DIM, (h + 1) * HEAD_DIM)
        qd_out[h] = jnp.concatenate([q_ref[:, at], grad_heads[:, at]], axis=1)
    for h in range(HEADS):
        arrival = r_qd.at[slot // 2]
        copy = remote(qd_out.at[h], qd_in.at[slot], s_qd.at[h], arrival, {"tm": base + OWNERS[h]})
        go_or_copy(slot == OWNERS[h], copy, qd_out.at[h], qd_in.at[slot], arrival)

    loads["stem"].wait()
    stem_in = stem_ref[...].astype(F32)
    normal_cdf = 0.5 * (1.0 + lax.erf(stem_in / math.sqrt(2.0)))
    density = jnp.exp(-0.5 * stem_in * stem_in) / math.sqrt(2.0 * math.pi)
    slope[...] = normal_cdf + stem_in * density
    activated = stem_in * normal_cdf
    position = (slot * ROWS + lax.broadcasted_iota(jnp.int32, (ROWS, D // 2), 0)).astype(F32)
    feature = lax.broadcasted_iota(jnp.int32, (ROWS, D // 2), 1).astype(F32)
    angle = position * jnp.exp(-math.log(10000.0) / (D // 2 - 1) * feature)
    embedded = activated + jnp.concatenate([jnp.sin(angle), jnp.cos(angle)], axis=1)
    centered = embedded - jnp.mean(embedded, axis=1, keepdims=True)
    inverse = lax.rsqrt(jnp.mean(centered * centered, axis=1, keepdims=True) + EPSILON)
    standard = centered * inverse
    xhat[...] = standard
    deviation[...] = inverse
    normed = (standard * gain_ref[...] + bias_ref[...]).astype(BF)
    for kind, source in enumerate((normed, go_ref[...])):
        for r in range(2):
            left_out[r, kind] = jnp.concatenate(
                [source[:, c * 2 * X_ROWS + r * X_ROWS : c * 2 * X_ROWS + (r + 1) * X_ROWS] for c in range(N_X)], axis=1
            )
    for place in range(QUAD):
        copy = remote(left_out.at[place % 2], left_in.at[t], s_left.at[place], r_left, at_quad(place))
        go_or_copy(t == place, copy, left_out.at[place % 2], left_in.at[t], r_left)

    head = jnp.int32(0)
    active = jnp.bool_(False)
    for h in range(HEADS):
        head = jnp.where(slot == OWNERS[h], h % GROUP, head)
        active = jnp.logical_or(active, slot == OWNERS[h])
    blocks = SEQ // BLOCK

    def back(buf, index, part, send_sem):
        place = QUAD * (index // 2) + 2 * low + lax.rem(index, 2)
        half = lax.rem(index, 2)
        return place, half, remote(
            buf.at[index], cols.at[part, half, head], send_sem.at[index], r_cols.at[part], {"tm": base + place}
        )

    def send_back(buf, index, part, send_sem):
        place, half, copy = back(buf, index, part, send_sem)
        go_or_copy(slot == place, copy, buf.at[index], cols.at[part, half, head], r_cols.at[part], keep=False)

    @pl.when(active)
    def _():
        limit = frames_ref[0, me // SPAN]
        landed(kv_in, r_kv)
        kv = kv_in[...].reshape(SEQ, PAIR)
        lane = lax.broadcasted_iota(jnp.int32, kv.shape, 1)
        row = lax.broadcasted_iota(jnp.int32, kv.shape, 0)
        fill = jnp.where(jnp.logical_and(lane == HEAD_DIM, 2 * row >= limit), NEG_FILL, 0.0)
        masked_k[...] = jnp.where(lane < HEAD_DIM, kv.astype(F32), fill).astype(BF)
        kv_t[...] = kv.T
        total[...] = jnp.zeros_like(total)
        scale = 1.0 / math.sqrt(HEAD_DIM)
        blane = lax.broadcasted_iota(jnp.int32, (BLOCK, PAIR), 1)
        brow = lax.broadcasted_iota(jnp.int32, (PAIR, BLOCK), 0)
        own = slot // QUAD

        def body(i, carry):
            step = i // 2
            near = lax.rem(own + step, 2) + 2 * lax.rem(own // 2 + step // 2, 2)
            at = 2 * near + lax.rem(i, 2)
            landed(qd_in.at[pl.ds(2 * at, 2)], r_qd.at[at])
            qd = qd_in[pl.ds(2 * at, 2)].reshape(BLOCK, PAIR).astype(F32)
            q_ones = jnp.where(blane < HEAD_DIM, qd * scale, jnp.where(blane == HEAD_DIM, 1.0, 0.0)).astype(BF)
            q_only = jnp.where(blane < HEAD_DIM, qd, 0.0).astype(BF)
            d_only = jnp.where(blane >= HEAD_DIM, qd, 0.0).astype(BF)
            scores = lax.dot_general(masked_k[...], q_ones, (((1,), (1,)), ((), ())), preferred_element_type=F32)
            top = jnp.max(scores, axis=0, keepdims=True)
            power = jnp.exp(scores - top)
            prob = power * (1.0 / jnp.sum(power, axis=0, keepdims=True))
            prob_b = prob.astype(BF)
            attn_t = jnp.dot(kv_t[...], prob_b, preferred_element_type=F32).astype(BF).astype(F32)
            delta = jnp.sum(jnp.where(brow >= HEAD_DIM, qd.T * attn_t, 0.0), axis=0, keepdims=True)
            grad_prob = lax.dot_general(
                kv_in[...].reshape(SEQ, PAIR), d_only, (((1,), (1,)), ((), ())), preferred_element_type=F32
            )
            dscore = (prob * (grad_prob - delta) * scale).astype(BF)
            dq_t = jnp.dot(kv_t[...], dscore, preferred_element_type=F32)
            ret_qo[at] = jnp.where(brow < HEAD_DIM, dq_t, attn_t).T.astype(BF)
            send_back(ret_qo, at, 0, s_qo)
            total[...] += jnp.dot(dscore, q_only, preferred_element_type=F32) + jnp.dot(
                prob_b, d_only, preferred_element_type=F32
            )
            return carry

        lax.fori_loop(0, blocks, body, 0)
        ret_kv[...] = total[...].astype(BF).reshape(blocks, BLOCK, PAIR)

        def send_kv_grads(i, carry):
            send_back(ret_kv, i, 1, s_dkv)
            return carry

        lax.fori_loop(0, blocks, send_kv_grads, 0)

    def spread(part):
        landed(cols.at[part, core], r_cols.at[part])
        go(remote(cols.at[part, core], cols.at[part, core], s_pair.at[part], r_pair.at[part], at_quad(2 * low + 1 - core)))
        for k in range(2):
            copy = remote(
                cols.at[part, core, :, pl.ds(k * ROWS, ROWS)], tok_in.at[part], s_tok.at[part, k], r_tok.at[part],
                at_quad(2 * core + k),
            )
            pl.when(core != low)(copy.start)
            pending.append((core == low, copy))

    tokens = QUAD * ROWS

    def rows_of(step, half):
        chunk = lax.rem(x + step, N_X)
        return pl.ds(pl.multiple_of(chunk * X_ROWS + half * HALF, 16), HALF)

    def multiply(part):
        landed(cols.at[part, 1 - core], r_pair.at[part])
        right = jnp.concatenate([cols[part, :, h].reshape(tokens, PAIR) for h in range(GROUP)], axis=1)
        even = lax.rem(lax.broadcasted_iota(jnp.int32, (128, PIECE), 1), PAIR) < HEAD_DIM
        for at in range(0, PIECE, 128):
            product = lax.dot_general(
                left_in[:, 0, :, at : at + 128].reshape(tokens, 128), right, (((0,), (0,)), ((), ())),
                preferred_element_type=F32,
            )
            if part == 0:
                other = lax.dot_general(
                    left_in[:, 1, :, at : at + 128].reshape(tokens, 128), right, (((0,), (0,)), ((), ())),
                    preferred_element_type=F32,
                )
                product = jnp.where(even, product, other)
            wide[part, at : at + 128] = product
            sends[part, at : at + 128] = product.astype(BF)

    turns = ((0, 1), (1, N_X - 1))

    def ring_start(part):
        for half, step in turns:
            go(remote(sends.at[part, rows_of(2, half)], first.at[part, half], s_first.at[part, half], r_first.at[part, half], at_x(step)))
        for half, step in turns:
            go(remote(sends.at[part, rows_of(step, 1 - half)], alone.at[part, 1 - half], s_alone.at[part, half], r_alone.at[part, 1 - half], at_x(step)))

    def ring_join(part):
        for half, step in turns:
            landed(first.at[part, half], r_first.at[part, half])
            joint_out[part, half] = (first[part, half].astype(F32) + wide[part, rows_of(step, half)]).astype(BF)
            go(remote(joint_out.at[part, half], joined.at[part, half], s_joined.at[part, half], r_joined.at[part, half], at_x(step)))

    def along_z(part):
        for half in range(2):
            landed(alone.at[part, half], r_alone.at[part, half])
            landed(joined.at[part, half], r_joined.at[part, half])
            summed = wide[part, rows_of(0, half)] + alone[part, half].astype(F32) + joined[part, half].astype(F32)
            for k in range(HALF // Z_ROWS):
                z_out[part, half * (HALF // Z_ROWS) + k] = jnp.concatenate(
                    [summed[k * Z_ROWS : (k + 1) * Z_ROWS], jnp.zeros((Z_PAD - Z_ROWS, PIECE), F32)], axis=0
                ).astype(BF)
        for k in range(QUAD):
            place = core * QUAD + k
            copy = remote(z_out.at[part, k], z_in.at[part, z], s_z.at[part, k], r_z.at[part], at_z(place))
            go_or_copy(place == z, copy, z_out.at[part, k], z_in.at[part, z], r_z.at[part])

    spread(0)
    landed(left_in, r_left)
    multiply(0)
    ring_start(0)
    spread(1)
    ring_join(0)
    multiply(1)
    ring_start(1)
    along_z(0)
    ring_join(1)

    loads["w_qkv"].wait()
    landed(tok_in.at[0], r_tok.at[0])
    landed(tok_in.at[1], r_tok.at[1])
    mine = pl.ds(pl.multiple_of(core * ROWS, ROWS), ROWS)

    def tile_of(part, h):
        here = cols[part, low, h % GROUP, mine]
        return jnp.where(low == h // GROUP, here, tok_in[part, h % GROUP])

    qo = [tile_of(0, h) for h in range(HEADS)]
    kv_grads = [tile_of(1, h) for h in range(HEADS)]
    grad_qkv = jnp.concatenate(
        [tile[:, :HEAD_DIM] for tile in qo]
        + [tile[:, :HEAD_DIM] for tile in kv_grads]
        + [tile[:, HEAD_DIM:] for tile in kv_grads],
        axis=1,
    )
    grad_normed = lax.dot_general(grad_qkv, w_qkv[...], (((1,), (1,)), ((), ())), preferred_element_type=F32)
    standard = xhat[...]
    for row, terms in enumerate((jnp.sum(grad_normed * standard, axis=0, keepdims=True), jnp.sum(grad_normed, axis=0, keepdims=True))):
        for k in range(TILES):
            norm_mid[0, row * TILES + k : row * TILES + k + 1] = terms[:, k * 128 : (k + 1) * 128]
    norm_mid[0, 2 * TILES :] = jnp.zeros((NORM_ROWS - 2 * TILES, 128), F32)
    for step in range(1, N_Z):
        go(remote(norm_mid.at[0], norm_a.at[z], s_na.at[step], r_na, at_z(lax.rem(z + step, N_Z))))
    norm_a[z] = norm_mid[0]
    along_z(1)
    gx = grad_normed * gain_ref[...]
    grad_x = go_ref[...].astype(F32) + deviation[...] * (
        gx - jnp.mean(gx, axis=1, keepdims=True) - standard * jnp.mean(gx * standard, axis=1, keepdims=True)
    )
    stem_out[0] = (grad_x * slope[...]).astype(BF)

    landed(norm_a.at[pl.ds(0, N_Z - 1)], r_na)
    norm_mid[1] = jnp.sum(norm_a[...], axis=0)
    for step in range(1, N_X):
        go(remote(norm_mid.at[1], norm_b.at[x], s_nb.at[step], r_nb, at_x(step)))
    norm_b[x] = norm_mid[1]
    landed(norm_b.at[pl.ds(0, N_X - 1)], r_nb)
    norm_mid[2] = jnp.sum(norm_b[...], axis=0)
    for step in range(1, 2 * QUAD):
        go(remote(norm_mid.at[2], norm_c.at[mine8], s_nc.at[step], r_nc, at_eight(step)))
    norm_c[mine8] = norm_mid[2]

    holder = core == z // QUAD
    source = side * 2 + low

    def last_copy(step):
        place = lax.rem(lax.rem(mine8 + step, 2 * QUAD), QUAD)
        return remote(last_out.at[place], last_in.at[source], s_last.at[step], r_last, at_eight(step))

    @pl.when(holder)
    def _():
        for part in range(2):
            landed(z_in.at[part], r_z.at[part])
            summed = jnp.sum(z_in[part].astype(F32), axis=0)
            for place in range(QUAD):
                last_out[place, part] = jnp.concatenate(
                    [summed[place * OUT_ROWS : (place + 1) * OUT_ROWS], jnp.zeros((OUT_PAD - OUT_ROWS, PIECE), F32)], axis=0
                )
        for step in range(1, 2 * QUAD):
            last_copy(step).start()
        pltpu.make_async_copy(last_out.at[t], last_in.at[source], r_last).start()

    landed(norm_c.at[pl.ds(0, 2 * QUAD - 1)], r_nc)
    norms = jnp.sum(norm_c[...], axis=0)
    for row in range(2):
        for k in range(TILES):
            norm_out[row : row + 1, k * 128 : (k + 1) * 128] = norms[row * TILES + k : row * TILES + k + 1]

    landed(last_in, r_last)
    quarters = [[], [], [], []]
    for g in range(2):
        both = last_in[g] + last_in[2 + g]
        for h in range(GROUP):
            for part, (a, b) in enumerate(((0, 3), (1, 2))):
                tile = both[part, :OUT_ROWS, h * PAIR : (h + 1) * PAIR]
                quarters[a].append(tile[:, :HEAD_DIM])
                quarters[b].append(tile[:, HEAD_DIM:])
    for k in range(4):
        out_ref[:, k * WIDTH : (k + 1) * WIDTH] = jnp.concatenate(quarters[k], axis=1)

    for entry in pending:
        if isinstance(entry, tuple):
            pl.when(jnp.logical_not(entry[0]))(entry[1].wait_send)
        else:
            entry.wait_send()

    @pl.when(holder)
    def _():
        for step in range(1, 2 * QUAD):
            last_copy(step).wait_send()

    @pl.when(active)
    def _():
        def drain(i, carry):
            for buf, part, sem in ((ret_qo, 0, s_qo), (ret_kv, 1, s_dkv)):
                place, half, copy = back(buf, i, part, sem)
                pl.when(slot != place)(copy.wait_send)
            return carry

        lax.fori_loop(0, blocks, drain, 0)


def local(stem_pre, gain, bias, w_attn, queries, keys, values, grad_out, frames):
    vmem, dma = pltpu.VMEM, pltpu.SemaphoreType.DMA
    tile = (ROWS, PAIR)
    blocks = SEQ // BLOCK
    anywhere, inside = pl.BlockSpec(memory_space=pl.ANY), pl.BlockSpec(memory_space=vmem)
    return pl.pallas_call(
        layer_kernel,
        out_shape=(
            jax.ShapeDtypeStruct((1, ROWS, D), BF),
            jax.ShapeDtypeStruct((OUT_ROWS, 4 * WIDTH), F32),
            jax.ShapeDtypeStruct((2, D), F32),
        ),
        in_specs=[anywhere, inside, inside, anywhere, anywhere, anywhere, anywhere, anywhere, pl.BlockSpec(memory_space=pltpu.SMEM)],
        out_specs=(inside, inside, inside),
        scratch_shapes=[
            vmem((ROWS, D), BF), vmem((D, WIDTH), BF), vmem((D, 3 * WIDTH), BF),
            vmem((ROWS, WIDTH), BF), vmem((ROWS, WIDTH), BF), vmem((ROWS, WIDTH), BF), vmem((ROWS, D), BF),
            vmem((HEADS,) + tile, BF), vmem((HEADS,) + tile, BF), vmem((SPAN,) + tile, BF), vmem((SPAN,) + tile, BF),
            vmem((blocks, BLOCK, PAIR), BF), vmem((blocks, BLOCK, PAIR), BF),
            vmem((SEQ, PAIR), BF), vmem((PAIR, SEQ), BF), vmem((SEQ, PAIR), F32),
            vmem((ROWS, D), F32), vmem((ROWS, D), F32), vmem((ROWS, 1), F32),
            vmem((2, 2, ROWS, D // 2), BF), vmem((QUAD, 2, ROWS, D // 2), BF),
            vmem((2, 2, GROUP, BLOCK, PAIR), BF), vmem((2, GROUP) + tile, BF),
            vmem((2, D // 2, PIECE), F32), vmem((2, D // 2, PIECE), BF),
            vmem((2, 2, HALF, PIECE), BF), vmem((2, 2, HALF, PIECE), BF), vmem((2, 2, HALF, PIECE), BF), vmem((2, 2, HALF, PIECE), BF),
            vmem((2, QUAD, Z_PAD, PIECE), BF), vmem((2, N_Z, Z_PAD, PIECE), BF),
            vmem((QUAD, 2, OUT_PAD, PIECE), F32), vmem((QUAD, 2, OUT_PAD, PIECE), F32),
            vmem((N_Z, NORM_ROWS, 128), F32), vmem((N_X, NORM_ROWS, 128), F32), vmem((2 * QUAD, NORM_ROWS, 128), F32),
            vmem((3, NORM_ROWS, 128), F32),
            dma((7,)), dma((HEADS,)), dma((HEADS,)), dma((blocks,)), dma((blocks,)), dma((QUAD,)), dma((2,)), dma((2, 2)),
            dma((2, 2)), dma((2, 2)), dma((2, 2)), dma((2, QUAD)), dma((2 * QUAD,)), dma((N_Z,)), dma((N_X,)), dma((2 * QUAD,)),
            dma, dma((blocks,)), dma((2,)), dma, dma((2,)), dma((2,)),
            dma((2, 2)), dma((2, 2)), dma((2, 2)), dma((2,)), dma, dma, dma, dma,
        ],
        compiler_params=pltpu.CompilerParams(
            collective_id=0, has_side_effects=True, vmem_limit_bytes=60 * 1024 * 1024
        ),
        name="layer_backward",
    )(stem_pre, gain.reshape(1, D), bias.reshape(1, D), w_attn, queries, keys, values, grad_out, frames)


def solution(mesh):
    placed = (
        P("batch", "tm", None),
        P(),
        P(),
        P(),
        P("batch", "tm", None),
        P("batch", "tm", None),
        P("batch", "tm", None),
        P("batch", "tm", None),
        P("batch", None),
    )
    return jax.shard_map(
        local,
        mesh=mesh,
        in_specs=placed,
        out_specs=(P("batch", "tm", None), P("tm", None), P()),
        check_vma=False,
    )
```

time: 1140 us -> 94.8 us (0.08)
  blocking collectives: 731 us -> 0 us
  waiting for transfers between devices: 312 us -> 0 us
  Pallas kernels: 0 us -> 86.7 us
  other arithmetic: 42.9 us -> 0 us
  matrix products: 27.5 us -> 0 us
    unnamed x1 -> x0, blocking collectives: 643 us -> none
    ppermute x8 -> x0, waiting for transfers between devices: 312 us -> none  [swapped(): lax.ppermute(array, axis, [(i, i ^ 1 << stride) for i in range(lax.axis_s...]
    psum x2 -> x0, blocking collectives: 87.8 us -> none  [the longest x1 79.3 us: local(): ln_grads = lax.psum(norm_correction_terms, ('tm', 'batch'))]
    pallas_call x0 -> x1, Pallas kernels: none -> 86.7 us  [local(): pl.pallas_call(layer_kernel, out_shape=(jax.ShapeDtypeStruct((1, ROWS, D)...]
    dot_general x10 -> x0, matrix products: 27.5 us -> none  [the longest x1 4.8 us: local(): jnp.einsum('qhd,khd->hqk', cot_heads, value_heads, preferred_element_type...]
  transfers between devices with their start and end apart: 8 -> 0, of which waited for: 7 -> 0; matrix products, arithmetic and copies ran while one was open for 1% -> 0% of each run, Pallas kernels for 0% -> 0%
where the time goes in v2:
time: 94.8 us; the launch traced here: 94.5 us
  Pallas kernels  86.7 us (91%)
  local copies, waits for them, and re-layouts  7.2 us (8%)
    pallas_call x1, Pallas kernels, local(): pl.pallas_call(layer_kernel, out_shape=(jax.ShapeDtypeStruct((1, ROWS, D)...  86.7 us
    unnamed x3, local copies, waits for them, and re-layouts  4.61 us

profile of v2, /device:TPU:1, one launch (start us, length us, event | category | flops | bytes accessed | tf_op | source)
XLA Modules:
  0.0 94.5 jit_solution(12402087247338007051)
XLA Ops:
  0.6 1.3 %reshape.12.gain_ref = f32[1,1280]{1,0:T(1,128)} reshape(f32[1280]{0:T(1024)} %param.10) | data formatting | bytes 10240 | tf_op jit(solution)/shard_map/reshape | solution.py:453
  1.9 1.3 %reshape.13.bias_ref = f32[1,1280]{1,0:T(1,128)} reshape(f32[1280]{0:T(1024)} %param.11) | data formatting | bytes 10240 | tf_op jit(solution)/shard_map/reshape | solution.py:453
  3.2 86.7 %layer_backward.1 = (bf16[1,128,1280]{2,1,0:T(8,128)(2,1)}, f32[10,2560]{1,0:T(8,128)}, f32[2,1280]{1,0:T(2,128)}) custom-call(bf16[1,128,1280]{2,1,0:T(8,128)(2,1)} %stem_hbm.1, f32[1,1280]{1,0:T(1,128)} %reshape.12.gain_ref, f32[1,1280]{1,0:T(1,128)} %reshape.13.bias_ref, bf16[1280,2560]{1,0:T(8,128)(2,1)} %w_hbm.1, bf16[1,128,640]{2,1,0:T(8,128)(2,1)} %q_hbm.1, ...), custom_call_target="tpu_custom_call" | custom-call | tf_op jit(solution)/shard_map/layer_backward/pallas_call | solution.py:420
  89.9 1.7 %copy.15 = bf16[1,128,1280]{2,1,0:T(8,128)(2,1)} copy(bf16[1,128,1280]{2,1,0:T(8,128)(2,1)} %get-tuple-element.6) | data formatting | bytes 655360
  91.6 1.6 %copy.16 = f32[10,2560]{1,0:T(8,128)} copy(f32[10,2560]{1,0:T(8,128)} %get-tuple-element.7) | data formatting | bytes 204800
  93.2 1.3 %copy.17 = f32[2,1280]{1,0:T(2,128)} copy(f32[2,1280]{1,0:T(2,128)} %get-tuple-element.8) | data formatting | bytes 20480

commit v3 on v2

--- a/solution.py
+++ b/solution.py
@@ -37,12 +37,12 @@
 
 def layer_kernel(
     stem_hbm, gain_ref, bias_ref, w_hbm, q_hbm, k_hbm, v_hbm, go_hbm, frames_ref,
-    stem_out, out_ref, norm_out,
+    stem_hbm_out, out_ref, norm_out,
     stem_ref, w_out, w_qkv, q_ref, k_ref, v_ref, go_ref,
     kv_out, qd_out, kv_in, qd_in, ret_qo, ret_kv, masked_k, kv_t, total,
     xhat, slope, deviation, left_out, left_in, cols, tok_in,
     wide, sends, first, joined, alone, joint_out, z_out, z_in, last_out, last_in,
-    norm_a, norm_b, norm_c, norm_mid,
+    norm_a, norm_b, norm_c, norm_mid, stem_out,
     s_load, s_kv, s_qd, s_qo, s_dkv, s_left, s_pair, s_tok, s_first, s_joined, s_alone, s_z, s_last,
     s_na, s_nb, s_nc,
     r_kv, r_qd, r_cols, r_left, r_pair, r_tok, r_first, r_joined, r_alone, r_z, r_last, r_na, r_nb, r_nc,
@@ -153,7 +153,7 @@
     standard = centered * inverse
     xhat[...] = standard
     deviation[...] = inverse
-    normed = (standard * gain_ref[...] + bias_ref[...]).astype(BF)
+    normed = (standard * gain_ref[...].reshape(1, D) + bias_ref[...].reshape(1, D)).astype(BF)
     for kind, source in enumerate((normed, go_ref[...])):
         for r in range(2):
             left_out[r, kind] = jnp.concatenate(
@@ -335,11 +335,13 @@
         go(remote(norm_mid.at[0], norm_a.at[z], s_na.at[step], r_na, at_z(lax.rem(z + step, N_Z))))
     norm_a[z] = norm_mid[0]
     along_z(1)
-    gx = grad_normed * gain_ref[...]
+    gx = grad_normed * gain_ref[...].reshape(1, D)
     grad_x = go_ref[...].astype(F32) + deviation[...] * (
         gx - jnp.mean(gx, axis=1, keepdims=True) - standard * jnp.mean(gx * standard, axis=1, keepdims=True)
     )
-    stem_out[0] = (grad_x * slope[...]).astype(BF)
+    stem_out[...] = (grad_x * slope[...]).astype(BF)
+    stem_copy = pltpu.make_async_copy(stem_out, stem_hbm_out.at[0], s_load.at[7])
+    stem_copy.start()
 
     landed(norm_a.at[pl.ds(0, N_Z - 1)], r_na)
     norm_mid[1] = jnp.sum(norm_a[...], axis=0)
@@ -367,7 +369,7 @@
             for place in range(QUAD):
                 last_out[place, part] = jnp.concatenate(
                     [summed[place * OUT_ROWS : (place + 1) * OUT_ROWS], jnp.zeros((OUT_PAD - OUT_ROWS, PIECE), F32)], axis=0
-                )
+                ).astype(BF)
         for step in range(1, 2 * QUAD):
             last_copy(step).start()
         pltpu.make_async_copy(last_out.at[t], last_in.at[source], r_last).start()
@@ -381,7 +383,7 @@
     landed(last_in, r_last)
     quarters = [[], [], [], []]
     for g in range(2):
-        both = last_in[g] + last_in[2 + g]
+        both = last_in[g].astype(F32) + last_in[2 + g].astype(F32)
         for h in range(GROUP):
             for part, (a, b) in enumerate(((0, 3), (1, 2))):
                 tile = both[part, :OUT_ROWS, h * PAIR : (h + 1) * PAIR]
@@ -390,6 +392,7 @@
     for k in range(4):
         out_ref[:, k * WIDTH : (k + 1) * WIDTH] = jnp.concatenate(quarters[k], axis=1)
 
+    stem_copy.wait()
     for entry in pending:
         if isinstance(entry, tuple):
             pl.when(jnp.logical_not(entry[0]))(entry[1].wait_send)
@@ -412,12 +415,38 @@
         lax.fori_loop(0, blocks, drain, 0)
 
 
+def copy_kernel(a, b, c, a_out, b_out, c_out, a_mid, b_mid, c_mid, sems):
+    routes = ((a, a_mid, a_out), (b, b_mid, b_out), (c, c_mid, c_out))
+    inward = [pltpu.make_async_copy(src, mid, sems.at[0, index]) for index, (src, mid, dst) in enumerate(routes)]
+    outward = [pltpu.make_async_copy(mid, dst, sems.at[1, index]) for index, (src, mid, dst) in enumerate(routes)]
+    for copy in inward:
+        copy.start()
+    for first, second in zip(inward, outward):
+        first.wait()
+        second.start()
+    for copy in outward:
+        copy.wait()
+
+
+def hand_on(*arrays):
+    anywhere = pl.BlockSpec(memory_space=pl.ANY)
+    return pl.pallas_call(
+        copy_kernel,
+        out_shape=tuple(jax.ShapeDtypeStruct(array.shape, array.dtype) for array in arrays),
+        in_specs=[anywhere] * 3,
+        out_specs=(anywhere,) * 3,
+        scratch_shapes=[pltpu.VMEM(array.shape, array.dtype) for array in arrays] + [pltpu.SemaphoreType.DMA((2, 3))],
+        compiler_params=pltpu.CompilerParams(vmem_limit_bytes=63 * 1024 * 1024),
+        name="hand_on",
+    )(*arrays)
+
+
 def local(stem_pre, gain, bias, w_attn, queries, keys, values, grad_out, frames):
     vmem, dma = pltpu.VMEM, pltpu.SemaphoreType.DMA
     tile = (ROWS, PAIR)
     blocks = SEQ // BLOCK
     anywhere, inside = pl.BlockSpec(memory_space=pl.ANY), pl.BlockSpec(memory_space=vmem)
-    return pl.pallas_call(
+    results = pl.pallas_call(
         layer_kernel,
         out_shape=(
             jax.ShapeDtypeStruct((1, ROWS, D), BF),
@@ -425,7 +454,7 @@
             jax.ShapeDtypeStruct((2, D), F32),
         ),
         in_specs=[anywhere, inside, inside, anywhere, anywhere, anywhere, anywhere, anywhere, pl.BlockSpec(memory_space=pltpu.SMEM)],
-        out_specs=(inside, inside, inside),
+        out_specs=(anywhere, inside, inside),
         scratch_shapes=[
             vmem((ROWS, D), BF), vmem((D, WIDTH), BF), vmem((D, 3 * WIDTH), BF),
             vmem((ROWS, WIDTH), BF), vmem((ROWS, WIDTH), BF), vmem((ROWS, WIDTH), BF), vmem((ROWS, D), BF),
@@ -438,10 +467,10 @@
             vmem((2, D // 2, PIECE), F32), vmem((2, D // 2, PIECE), BF),
             vmem((2, 2, HALF, PIECE), BF), vmem((2, 2, HALF, PIECE), BF), vmem((2, 2, HALF, PIECE), BF), vmem((2, 2, HALF, PIECE), BF),
             vmem((2, QUAD, Z_PAD, PIECE), BF), vmem((2, N_Z, Z_PAD, PIECE), BF),
-            vmem((QUAD, 2, OUT_PAD, PIECE), F32), vmem((QUAD, 2, OUT_PAD, PIECE), F32),
+            vmem((QUAD, 2, OUT_PAD, PIECE), BF), vmem((QUAD, 2, OUT_PAD, PIECE), BF),
             vmem((N_Z, NORM_ROWS, 128), F32), vmem((N_X, NORM_ROWS, 128), F32), vmem((2 * QUAD, NORM_ROWS, 128), F32),
-            vmem((3, NORM_ROWS, 128), F32),
-            dma((7,)), dma((HEADS,)), dma((HEADS,)), dma((blocks,)), dma((blocks,)), dma((QUAD,)), dma((2,)), dma((2, 2)),
+            vmem((3, NORM_ROWS, 128), F32), vmem((ROWS, D), BF),
+            dma((8,)), dma((HEADS,)), dma((HEADS,)), dma((blocks,)), dma((blocks,)), dma((QUAD,)), dma((2,)), dma((2, 2)),
             dma((2, 2)), dma((2, 2)), dma((2, 2)), dma((2, QUAD)), dma((2 * QUAD,)), dma((N_Z,)), dma((N_X,)), dma((2 * QUAD,)),
             dma, dma((blocks,)), dma((2,)), dma, dma((2,)), dma((2,)),
             dma((2, 2)), dma((2, 2)), dma((2, 2)), dma((2,)), dma, dma, dma, dma,
@@ -450,7 +479,8 @@
             collective_id=0, has_side_effects=True, vmem_limit_bytes=60 * 1024 * 1024
         ),
         name="layer_backward",
-    )(stem_pre, gain.reshape(1, D), bias.reshape(1, D), w_attn, queries, keys, values, grad_out, frames)
+    )(stem_pre, gain, bias, w_attn, queries, keys, values, grad_out, frames)
+    return hand_on(*results)
 
 
 def solution(mesh):

time: 94.8 us -> 87.5 us (0.923)
  local copies, waits for them, and re-layouts: 7.2 us -> 0 us
    unnamed x3 -> x0, local copies, waits for them, and re-layouts: 4.61 us -> none
    reshape x2 -> x0, local copies, waits for them, and re-layouts: 2.59 us -> none  [the longest x1 1.29 us: local(): gain.reshape(1, D)]
    pallas_call x0 -> x1, Pallas kernels: none -> 1.8 us  [hand_on(): pl.pallas_call(copy_kernel, out_shape=tuple((jax.ShapeDtypeStruct(array.s...]
    pallas_call x1, Pallas kernels: 86.7 us -> 84.9 us  [local(): pl.pallas_call(layer_kernel, out_shape=(jax.ShapeDtypeStruct((1, ROWS, D)...]
where the time goes in v3:
time: 87.5 us; the launch traced here: 87.4 us
  Pallas kernels  86.7 us (99%)
    pallas_call x1, Pallas kernels, local(): pl.pallas_call(layer_kernel, out_shape=(jax.ShapeDtypeStruct((1, ROWS, D)...  84.9 us
    pallas_call x1, Pallas kernels, hand_on(): pl.pallas_call(copy_kernel, out_shape=tuple((jax.ShapeDtypeStruct(array.s...  1.8 us

profile of v3, /device:TPU:1, one launch (start us, length us, event | category | flops | bytes accessed | tf_op | source)
XLA Modules:
  0.0 87.4 jit_solution(13115285130218649444)
XLA Ops:
  0.6 84.9 %layer_backward.1 = (bf16[1,128,1280]{2,1,0:T(8,128)(2,1)}, f32[10,2560]{1,0:T(8,128)}, f32[2,1280]{1,0:T(2,128)}) custom-call(bf16[1,128,1280]{2,1,0:T(8,128)(2,1)} %stem_hbm.1, f32[1280]{0:T(1024)} %gain_ref.1, f32[1280]{0:T(1024)} %bias_ref.1, bf16[1280,2560]{1,0:T(8,128)(2,1)} %w_hbm.1, bf16[1,128,640]{2,1,0:T(8,128)(2,1)} %q_hbm.1, ...), custom_call_target="tpu_custom_call" | custom-call | tf_op jit(solution)/shard_map/layer_backward/pallas_call | solution.py:449
  85.6 1.8 %hand_on.1 = (bf16[1,128,1280]{2,1,0:T(8,128)(2,1)}, f32[10,2560]{1,0:T(8,128)}, f32[2,1280]{1,0:T(2,128)}) custom-call(bf16[1,128,1280]{2,1,0:T(8,128)(2,1)} %get-tuple-element.6.a, f32[10,2560]{1,0:T(8,128)} %get-tuple-element.7.b, f32[2,1280]{1,0:T(2,128)} %get-tuple-element.8.c), custom_call_target="tpu_custom_call" | custom-call | tf_op jit(solution)/shard_map/hand_on/pallas_call | solution.py:433

commit v4 on v3

--- a/solution.py
+++ b/solution.py
@@ -32,6 +32,7 @@
 OUT_PAD = 16
 NORM_ROWS = 24
 TILES = D // 128
+CHUNK = 1024
 BF, F32 = jnp.bfloat16, jnp.float32
 
 
@@ -39,7 +40,7 @@
     stem_hbm, gain_ref, bias_ref, w_hbm, q_hbm, k_hbm, v_hbm, go_hbm, frames_ref,
     stem_hbm_out, out_ref, norm_out,
     stem_ref, w_out, w_qkv, q_ref, k_ref, v_ref, go_ref,
-    kv_out, qd_out, kv_in, qd_in, ret_qo, ret_kv, masked_k, kv_t, total,
+    kv_out, qd_out, kv_in, qd_in, ret_qo, ret_kv, masked_k, kv_t, total, scores, powers,
     xhat, slope, deviation, left_out, left_in, cols, tok_in,
     wide, sends, first, joined, alone, joint_out, z_out, z_in, last_out, last_in,
     norm_a, norm_b, norm_c, norm_mid, stem_out,
@@ -194,7 +195,6 @@
         total[...] = jnp.zeros_like(total)
         scale = 1.0 / math.sqrt(HEAD_DIM)
         blane = lax.broadcasted_iota(jnp.int32, (BLOCK, PAIR), 1)
-        brow = lax.broadcasted_iota(jnp.int32, (PAIR, BLOCK), 0)
         own = slot // QUAD
 
         def body(i, carry):
@@ -205,24 +205,43 @@
             qd = qd_in[pl.ds(2 * at, 2)].reshape(BLOCK, PAIR).astype(F32)
             q_ones = jnp.where(blane < HEAD_DIM, qd * scale, jnp.where(blane == HEAD_DIM, 1.0, 0.0)).astype(BF)
             q_only = jnp.where(blane < HEAD_DIM, qd, 0.0).astype(BF)
-            d_only = jnp.where(blane >= HEAD_DIM, qd, 0.0).astype(BF)
-            scores = lax.dot_general(masked_k[...], q_ones, (((1,), (1,)), ((), ())), preferred_element_type=F32)
-            top = jnp.max(scores, axis=0, keepdims=True)
-            power = jnp.exp(scores - top)
-            prob = power * (1.0 / jnp.sum(power, axis=0, keepdims=True))
-            prob_b = prob.astype(BF)
-            attn_t = jnp.dot(kv_t[...], prob_b, preferred_element_type=F32).astype(BF).astype(F32)
-            delta = jnp.sum(jnp.where(brow >= HEAD_DIM, qd.T * attn_t, 0.0), axis=0, keepdims=True)
-            grad_prob = lax.dot_general(
-                kv_in[...].reshape(SEQ, PAIR), d_only, (((1,), (1,)), ((), ())), preferred_element_type=F32
-            )
-            dscore = (prob * (grad_prob - delta) * scale).astype(BF)
-            dq_t = jnp.dot(kv_t[...], dscore, preferred_element_type=F32)
-            ret_qo[at] = jnp.where(brow < HEAD_DIM, dq_t, attn_t).T.astype(BF)
+            top = jnp.full((8, BLOCK), NEG_FILL, F32)
+            for c in range(0, SEQ, CHUNK):
+                part = lax.dot_general(
+                    masked_k[c : c + CHUNK], q_ones, (((1,), (1,)), ((), ())), preferred_element_type=F32
+                )
+                scores[c : c + CHUNK] = part
+                top = jnp.maximum(top, jnp.max(part.reshape(CHUNK // 8, 8, BLOCK), axis=0))
+            top = jnp.max(top, axis=0, keepdims=True)
+            mass = jnp.zeros((8, BLOCK), F32)
+            attn_t = jnp.zeros((HEAD_DIM, BLOCK), F32)
+            for c in range(0, SEQ, CHUNK):
+                power = jnp.exp(scores[c : c + CHUNK] - top)
+                mass = mass + jnp.sum(power.reshape(CHUNK // 8, 8, BLOCK), axis=0)
+                power_b = power.astype(BF)
+                powers[c : c + CHUNK] = power_b
+                attn_t = attn_t + jnp.dot(kv_t[HEAD_DIM:, c : c + CHUNK], power_b, preferred_element_type=F32)
+            inverse_mass = 1.0 / jnp.sum(mass, axis=0, keepdims=True)
+            attn_t = (attn_t * inverse_mass).astype(BF).astype(F32)
+            shared_t = qd.T[HEAD_DIM:] * inverse_mass
+            shared = jnp.concatenate([jnp.zeros((HEAD_DIM, BLOCK), F32), shared_t], axis=0).T
+            d_only = shared.astype(BF)
+            d_scaled = (shared * scale).astype(BF)
+            delta = scale * jnp.sum(shared_t.astype(BF).astype(F32) * attn_t, axis=0, keepdims=True)
+            dq_t = jnp.zeros((HEAD_DIM, BLOCK), F32)
+            for c in range(0, SEQ, CHUNK):
+                grad_prob = lax.dot_general(
+                    kv_in[c // ROWS : (c + CHUNK) // ROWS].reshape(CHUNK, PAIR), d_scaled, (((1,), (1,)), ((), ())),
+                    preferred_element_type=F32,
+                )
+                power_b = powers[c : c + CHUNK]
+                dscore = (power_b.astype(F32) * (grad_prob - delta)).astype(BF)
+                dq_t = dq_t + jnp.dot(kv_t[:HEAD_DIM, c : c + CHUNK], dscore, preferred_element_type=F32)
+                total[c : c + CHUNK] += jnp.dot(dscore, q_only, preferred_element_type=F32) + jnp.dot(
+                    power_b, d_only, preferred_element_type=F32
+                )
+            ret_qo[at] = jnp.concatenate([dq_t, attn_t], axis=0).T.astype(BF)
             send_back(ret_qo, at, 0, s_qo)
-            total[...] += jnp.dot(dscore, q_only, preferred_element_type=F32) + jnp.dot(
-                prob_b, d_only, preferred_element_type=F32
-            )
             return carry
 
         lax.fori_loop(0, blocks, body, 0)
@@ -460,7 +479,7 @@
             vmem((ROWS, WIDTH), BF), vmem((ROWS, WIDTH), BF), vmem((ROWS, WIDTH), BF), vmem((ROWS, D), BF),
             vmem((HEADS,) + tile, BF), vmem((HEADS,) + tile, BF), vmem((SPAN,) + tile, BF), vmem((SPAN,) + tile, BF),
             vmem((blocks, BLOCK, PAIR), BF), vmem((blocks, BLOCK, PAIR), BF),
-            vmem((SEQ, PAIR), BF), vmem((PAIR, SEQ), BF), vmem((SEQ, PAIR), F32),
+            vmem((SEQ, PAIR), BF), vmem((PAIR, SEQ), BF), vmem((SEQ, PAIR), F32), vmem((SEQ, BLOCK), F32), vmem((SEQ, BLOCK), BF),
             vmem((ROWS, D), F32), vmem((ROWS, D), F32), vmem((ROWS, 1), F32),
             vmem((2, 2, ROWS, D // 2), BF), vmem((QUAD, 2, ROWS, D // 2), BF),
             vmem((2, 2, GROUP, BLOCK, PAIR), BF), vmem((2, GROUP) + tile, BF),

time: 87.5 us -> 81.7 us (0.934)
  Pallas kernels: 86.7 us -> 80.9 us
    pallas_call x1, Pallas kernels: 84.9 us -> 79.1 us  [local(): pl.pallas_call(layer_kernel, out_shape=(jax.ShapeDtypeStruct((1, ROWS, D)...]
where the time goes in v4:
time: 81.7 us; the launch traced here: 81.5 us
  Pallas kernels  80.9 us (99%)
    pallas_call x1, Pallas kernels, local(): pl.pallas_call(layer_kernel, out_shape=(jax.ShapeDtypeStruct((1, ROWS, D)...  79.1 us
    pallas_call x1, Pallas kernels, hand_on(): pl.pallas_call(copy_kernel, out_shape=tuple((jax.ShapeDtypeStruct(array.s...  1.8 us

profile of v4, /device:TPU:1, one launch (start us, length us, event | category | flops | bytes accessed | tf_op | source)
XLA Modules:
  0.0 81.5 jit_solution(3065545898281366732)
XLA Ops:
  0.6 79.1 %layer_backward.1 = (bf16[1,128,1280]{2,1,0:T(8,128)(2,1)}, f32[10,2560]{1,0:T(8,128)}, f32[2,1280]{1,0:T(2,128)}) custom-call(bf16[1,128,1280]{2,1,0:T(8,128)(2,1)} %stem_hbm.1, f32[1280]{0:T(1024)} %gain_ref.1, f32[1280]{0:T(1024)} %bias_ref.1, bf16[1280,2560]{1,0:T(8,128)(2,1)} %w_hbm.1, bf16[1,128,640]{2,1,0:T(8,128)(2,1)} %q_hbm.1, ...), custom_call_target="tpu_custom_call" | custom-call | tf_op jit(solution)/shard_map/layer_backward/pallas_call | solution.py:468
  79.7 1.8 %hand_on.1 = (bf16[1,128,1280]{2,1,0:T(8,128)(2,1)}, f32[10,2560]{1,0:T(8,128)}, f32[2,1280]{1,0:T(2,128)}) custom-call(bf16[1,128,1280]{2,1,0:T(8,128)(2,1)} %get-tuple-element.6.a, f32[10,2560]{1,0:T(8,128)} %get-tuple-element.7.b, f32[2,1280]{1,0:T(2,128)} %get-tuple-element.8.c), custom_call_target="tpu_custom_call" | custom-call | tf_op jit(solution)/shard_map/hand_on/pallas_call | solution.py:452

commit v5 on v4

--- a/solution.py
+++ b/solution.py
@@ -199,6 +199,7 @@
 
         def body(i, carry):
             step = i // 2
+            step = jnp.where(step == 0, 0, jnp.where(step == 1, 2, jnp.where(step == 2, 3, 1)))
             near = lax.rem(own + step, 2) + 2 * lax.rem(own // 2 + step // 2, 2)
             at = 2 * near + lax.rem(i, 2)
             landed(qd_in.at[pl.ds(2 * at, 2)], r_qd.at[at])
@@ -248,7 +249,10 @@
         ret_kv[...] = total[...].astype(BF).reshape(blocks, BLOCK, PAIR)
 
         def send_kv_grads(i, carry):
-            send_back(ret_kv, i, 1, s_dkv)
+            step = i // 2
+            step = jnp.where(step == 0, 2, jnp.where(step == 1, 3, jnp.where(step == 2, 1, 0)))
+            near = lax.rem(own + step, 2) + 2 * lax.rem(own // 2 + step // 2, 2)
+            send_back(ret_kv, 2 * near + lax.rem(i, 2), 1, s_dkv)
             return carry
 
         lax.fori_loop(0, blocks, send_kv_grads, 0)
@@ -324,8 +328,6 @@
     ring_join(0)
     multiply(1)
     ring_start(1)
-    along_z(0)
-    ring_join(1)
 
     loads["w_qkv"].wait()
     landed(tok_in.at[0], r_tok.at[0])
@@ -353,7 +355,8 @@
     for step in range(1, N_Z):
         go(remote(norm_mid.at[0], norm_a.at[z], s_na.at[step], r_na, at_z(lax.rem(z + step, N_Z))))
     norm_a[z] = norm_mid[0]
-    along_z(1)
+    along_z(0)
+    ring_join(1)
     gx = grad_normed * gain_ref[...].reshape(1, D)
     grad_x = go_ref[...].astype(F32) + deviation[...] * (
         gx - jnp.mean(gx, axis=1, keepdims=True) - standard * jnp.mean(gx * standard, axis=1, keepdims=True)
@@ -361,6 +364,7 @@
     stem_out[...] = (grad_x * slope[...]).astype(BF)
     stem_copy = pltpu.make_async_copy(stem_out, stem_hbm_out.at[0], s_load.at[7])
     stem_copy.start()
+    along_z(1)
 
     landed(norm_a.at[pl.ds(0, N_Z - 1)], r_na)
     norm_mid[1] = jnp.sum(norm_a[...], axis=0)

time: 81.7 us -> 79.6 us (0.974)
  Pallas kernels: 80.9 us -> 78.8 us
    pallas_call x1, Pallas kernels: 79.1 us -> 77 us  [local(): pl.pallas_call(layer_kernel, out_shape=(jax.ShapeDtypeStruct((1, ROWS, D)...]
where the time goes in v5:
time: 79.6 us; the launch traced here: 79.5 us
  Pallas kernels  78.8 us (99%)
    pallas_call x1, Pallas kernels, local(): pl.pallas_call(layer_kernel, out_shape=(jax.ShapeDtypeStruct((1, ROWS, D)...  77 us
    pallas_call x1, Pallas kernels, hand_on(): pl.pallas_call(copy_kernel, out_shape=tuple((jax.ShapeDtypeStruct(array.s...  1.8 us

profile of v5, /device:TPU:1, one launch (start us, length us, event | category | flops | bytes accessed | tf_op | source)
XLA Modules:
  0.0 79.5 jit_solution(4887119055564915624)
XLA Ops:
  0.6 77.0 %layer_backward.1 = (bf16[1,128,1280]{2,1,0:T(8,128)(2,1)}, f32[10,2560]{1,0:T(8,128)}, f32[2,1280]{1,0:T(2,128)}) custom-call(bf16[1,128,1280]{2,1,0:T(8,128)(2,1)} %stem_hbm.1, f32[1280]{0:T(1024)} %gain_ref.1, f32[1280]{0:T(1024)} %bias_ref.1, bf16[1280,2560]{1,0:T(8,128)(2,1)} %w_hbm.1, bf16[1,128,640]{2,1,0:T(8,128)(2,1)} %q_hbm.1, ...), custom_call_target="tpu_custom_call" | custom-call | tf_op jit(solution)/shard_map/layer_backward/pallas_call | solution.py:472
  77.7 1.8 %hand_on.1 = (bf16[1,128,1280]{2,1,0:T(8,128)(2,1)}, f32[10,2560]{1,0:T(8,128)}, f32[2,1280]{1,0:T(2,128)}) custom-call(bf16[1,128,1280]{2,1,0:T(8,128)(2,1)} %get-tuple-element.6.a, f32[10,2560]{1,0:T(8,128)} %get-tuple-element.7.b, f32[2,1280]{1,0:T(2,128)} %get-tuple-element.8.c), custom_call_target="tpu_custom_call" | custom-call | tf_op jit(solution)/shard_map/hand_on/pallas_call | solution.py:456
